TPU v7x, 32 devices: a whole 2x2x4 slice. The times are simulated.
32 devices in a mesh: fsdp: 8 (over z, y), sub: 4 (over x, core).
Axes of the slice: x: 2, y: 2, z: 4, core: 2. Of those that a mesh axis runs over, the one named last changes fastest.
Arguments:
- images: bfloat16 [128, 256, 768], P(('fsdp', 'sub')), may hold values from -6 to 6
- counts: int32 [128], P(('fsdp', 'sub')), may hold values from 18 to 256, as said below
- joint_weight: bfloat16 [768, 2304], P('fsdp', 'sub'), may hold values from -0.21875 to 0.21875
- out_weight: bfloat16 [768, 768], P('fsdp', 'sub'), may hold values from -1.75 to 1.75
- up_weight: bfloat16 [768, 3072], P('fsdp', 'sub'), may hold values from -0.21875 to 0.21875
- down_weight: bfloat16 [3072, 768], P('fsdp', 'sub'), may hold values from -0.109375 to 0.109375
- first_gain: bfloat16 [768], P(('fsdp', 'sub')), may hold values from 0.099609375 to 1.8984375
- first_shift: bfloat16 [768], P(('fsdp', 'sub')), may hold values from -3 to 3
- query_bias: bfloat16 [768], P(('fsdp', 'sub')), may hold values from -3 to 3
- value_bias: bfloat16 [768], P(('fsdp', 'sub')), may hold values from -3 to 3
- out_bias: bfloat16 [768], P(('fsdp', 'sub')), may hold values from -2 to 2
- first_scale: bfloat16 [768], P(('fsdp', 'sub')), may hold values from 0.5 to 1.5
- second_gain: bfloat16 [768], P(('fsdp', 'sub')), may hold values from 0.099609375 to 1.8984375
- second_shift: bfloat16 [768], P(('fsdp', 'sub')), may hold values from -3 to 3
- up_bias: bfloat16 [3072], P(('fsdp', 'sub')), may hold values from -3 to 3
- down_bias: bfloat16 [768], P(('fsdp', 'sub')), may hold values from -2 to 2
- second_scale: bfloat16 [768], P(('fsdp', 'sub')), may hold values from 0.5 to 1.5
- cotangent: bfloat16 [128, 256, 768], P(('fsdp', 'sub')), may hold values from -6 to 6
Outputs:
- block_out: bfloat16 [128, 256, 768], P(('fsdp', 'sub'))
- image_grad: float32 [128, 256, 768], P(('fsdp', 'sub'))
- joint_grad: float32 [768, 2304], P('fsdp', 'sub')
- out_grad: float32 [768, 768], P('fsdp', 'sub')
- up_grad: float32 [768, 3072], P('fsdp', 'sub')
- down_grad: float32 [3072, 768], P('fsdp', 'sub')
- first_gain_grad: float32 [768], P(('fsdp', 'sub'))
- first_shift_grad: float32 [768], P(('fsdp', 'sub'))
- query_bias_grad: float32 [768], P(('fsdp', 'sub'))
- value_bias_grad: float32 [768], P(('fsdp', 'sub'))
- out_bias_grad: float32 [768], P(('fsdp', 'sub'))
- first_scale_grad: float32 [768], P(('fsdp', 'sub'))
- second_gain_grad: float32 [768], P(('fsdp', 'sub'))
- second_shift_grad: float32 [768], P(('fsdp', 'sub'))
- up_bias_grad: float32 [3072], P(('fsdp', 'sub'))
- down_bias_grad: float32 [768], P(('fsdp', 'sub'))
- second_scale_grad: float32 [768], P(('fsdp', 'sub'))
Inputs may be any that keep to these rules, and one draw needn't show every extreme that they name: `counts`: image 0 is always full.
All inputs are finite; a program needn't handle non-finite values.
Results may differ from a plain program's by a relative error of at most 0.02.
Values may be sent and summed in bfloat16 or wider, within the bound.
No kernel may reach another device: no remote copies, remote signals or barrier semaphores. Data moves between devices by JAX's collectives and lax.ppermute only.
A program may use at most 192 MiB of HBM per device.

v0:
```python
import math

import jax
import jax.numpy as jnp
from jax import lax
from jax.sharding import PartitionSpec as P

HD = 64


EPS = 1e-06
NEGATIVE = -1e30


def normalize(rows):
    centre = rows - jnp.mean(rows, axis=-1, keepdims=True)
    spread = jnp.mean(centre * centre, axis=-1, keepdims=True)
    inverse = lax.rsqrt(spread + EPS)
    return (centre * inverse, inverse)


def norm_back(upstream, normed, inverse, gain):
    gain_grad = jnp.sum(upstream * normed, axis=0)
    shift_grad = jnp.sum(upstream, axis=0)
    scaled = upstream * gain
    inner = (
        scaled
        - jnp.mean(scaled, axis=-1, keepdims=True)
        - normed * jnp.mean(scaled * normed, axis=-1, keepdims=True)
    )
    return (inverse * inner, gain_grad, shift_grad)


def column_sum(values):
    return jnp.sum(values.astype(jnp.float32), axis=0)


def outer_sum(left, right):
    return jnp.einsum("na,nb->ab", left, right, preferred_element_type=jnp.float32)


def back_product(left, weight):
    return jnp.einsum("nb,ab->na", left, weight, preferred_element_type=jnp.float32)


def shards(
    images,
    counts,
    joint_weight,
    out_weight,
    up_weight,
    down_weight,
    first_gain,
    first_shift,
    query_bias,
    value_bias,
    out_bias,
    first_scale,
    second_gain,
    second_shift,
    up_bias,
    down_bias,
    second_scale,
    cotangent,
):
    columns = (
        lax.all_gather(joint_weight, "sub", axis=1, tiled=True),
        lax.all_gather(out_weight, "sub", axis=1, tiled=True),
        lax.all_gather(up_weight, "sub", axis=1, tiled=True),
        lax.all_gather(down_weight, "sub", axis=1, tiled=True),
        lax.all_gather(first_gain, "sub", axis=0, tiled=True),
        lax.all_gather(first_shift, "sub", axis=0, tiled=True),
        lax.all_gather(query_bias, "sub", axis=0, tiled=True),
        lax.all_gather(value_bias, "sub", axis=0, tiled=True),
        lax.all_gather(out_bias, "sub", axis=0, tiled=True),
        lax.all_gather(first_scale, "sub", axis=0, tiled=True),
        lax.all_gather(second_gain, "sub", axis=0, tiled=True),
        lax.all_gather(second_shift, "sub", axis=0, tiled=True),
        lax.all_gather(up_bias, "sub", axis=0, tiled=True),
        lax.all_gather(down_bias, "sub", axis=0, tiled=True),
        lax.all_gather(second_scale, "sub", axis=0, tiled=True),
    )
    gathered = (
        lax.all_gather(columns[0], "fsdp", axis=0, tiled=True),
        lax.all_gather(columns[1], "fsdp", axis=0, tiled=True),
        lax.all_gather(columns[2], "fsdp", axis=0, tiled=True),
        lax.all_gather(columns[3], "fsdp", axis=0, tiled=True),
        lax.all_gather(columns[4], "fsdp", axis=0, tiled=True),
        lax.all_gather(columns[5], "fsdp", axis=0, tiled=True),
        lax.all_gather(columns[6], "fsdp", axis=0, tiled=True),
        lax.all_gather(columns[7], "fsdp", axis=0, tiled=True),
        lax.all_gather(columns[8], "fsdp", axis=0, tiled=True),
        lax.all_gather(columns[9], "fsdp", axis=0, tiled=True),
        lax.all_gather(columns[10], "fsdp", axis=0, tiled=True),
        lax.all_gather(columns[11], "fsdp", axis=0, tiled=True),
        lax.all_gather(columns[12], "fsdp", axis=0, tiled=True),
        lax.all_gather(columns[13], "fsdp", axis=0, tiled=True),
        lax.all_gather(columns[14], "fsdp", axis=0, tiled=True),
    )
    joint, out_full, up_full, down_full = (gathered[0], gathered[1], gathered[2], gathered[3])
    (
        gain_one,
        shift_one,
        query_add,
        value_add,
        out_add,
        scale_one,
        gain_two,
        shift_two,
        up_add,
        down_add,
        scale_two,
    ) = tuple((vector.astype(jnp.float32) for vector in gathered[4:]))
    count, length, width = images.shape
    heads = width // HD
    factor = 1.0 / math.sqrt(HD)
    positions = jnp.arange(length, dtype=jnp.int32)
    valid = positions[None, :] < counts[:, None]
    row_mask = valid.reshape(-1, 1).astype(jnp.float32)
    key_mask = valid[:, None, None, :]
    shape_four = (count, length, heads, HD)
    rows = images.reshape(-1, width).astype(jnp.float32)
    normed_one, inverse_one = normalize(rows)
    first_in = (normed_one * gain_one + shift_one).astype(jnp.bfloat16)
    joint_bias = jnp.concatenate([query_add, jnp.zeros_like(query_add), value_add])
    mixed = (jnp.dot(first_in, joint, preferred_element_type=jnp.float32) + joint_bias).astype(
        jnp.bfloat16
    )
    query = mixed[:, :width].reshape(shape_four)
    keys_in = mixed[:, width : 2 * width].reshape(shape_four)
    values_in = mixed[:, 2 * width :].reshape(shape_four)
    scores = (
        jnp.einsum("bqhd,bkhd->bhqk", query, keys_in, preferred_element_type=jnp.float32) * factor
    )
    scores = jnp.where(key_mask, scores, NEGATIVE)
    largest = jnp.max(scores, axis=-1, keepdims=True)
    expon = jnp.exp(scores - largest)
    probs = expon / jnp.sum(expon, axis=-1, keepdims=True)
    probs_low = probs.astype(jnp.bfloat16)
    attended = jnp.einsum(
        "bhqk,bkhd->bqhd", probs_low, values_in, preferred_element_type=jnp.float32
    )
    attended = attended.reshape(-1, width).astype(jnp.bfloat16)
    branch = jnp.dot(attended, out_full, preferred_element_type=jnp.float32) + out_add
    resid = rows + scale_one * branch
    normed_two, inverse_two = normalize(resid)
    second_in = (normed_two * gain_two + shift_two).astype(jnp.bfloat16)
    pre_act = jnp.dot(second_in, up_full, preferred_element_type=jnp.float32) + up_add
    hidden = jax.nn.gelu(pre_act, approximate=False).astype(jnp.bfloat16)
    feed_out = jnp.dot(hidden, down_full, preferred_element_type=jnp.float32) + down_add
    block_out = (
        ((resid + scale_two * feed_out) * row_mask).reshape(images.shape).astype(jnp.bfloat16)
    )
    again_columns = (
        lax.all_gather(joint_weight, "sub", axis=1, tiled=True),
        lax.all_gather(out_weight, "sub", axis=1, tiled=True),
        lax.all_gather(up_weight, "sub", axis=1, tiled=True),
        lax.all_gather(down_weight, "sub", axis=1, tiled=True),
    )
    again = (
        lax.all_gather(again_columns[0], "fsdp", axis=0, tiled=True),
        lax.all_gather(again_columns[1], "fsdp", axis=0, tiled=True),
        lax.all_gather(again_columns[2], "fsdp", axis=0, tiled=True),
        lax.all_gather(again_columns[3], "fsdp", axis=0, tiled=True),
    )
    joint_back, out_back, up_back, down_back = (again[0], again[1], again[2], again[3])
    upstream = cotangent.reshape(-1, width).astype(jnp.float32) * row_mask
    scale_two_grad = jnp.sum(upstream * feed_out, axis=0)
    dfeed = (upstream * scale_two).astype(jnp.bfloat16)
    down_bias_grad = column_sum(dfeed)
    down_grad = outer_sum(hidden, dfeed)
    dhidden = back_product(dfeed, down_back)
    cumul = 0.5 * (1.0 + jax.scipy.special.erf(pre_act / math.sqrt(2.0)))
    density = jnp.exp(-0.5 * pre_act * pre_act) / math.sqrt(2.0 * math.pi)
    dpre = (dhidden * (cumul + pre_act * density)).astype(jnp.bfloat16)
    up_bias_grad = column_sum(dpre)
    up_grad = outer_sum(second_in, dpre)
    dsecond = back_product(dpre, up_back)
    dnorm_two, gain_two_grad, shift_two_grad = norm_back(dsecond, normed_two, inverse_two, gain_two)
    dresid = upstream + dnorm_two
    scale_one_grad = jnp.sum(dresid * branch, axis=0)
    dbranch = (dresid * scale_one).astype(jnp.bfloat16)
    out_bias_grad = column_sum(dbranch)
    out_grad = outer_sum(attended, dbranch)
    dattended = back_product(dbranch, out_back).astype(jnp.bfloat16).reshape(shape_four)
    dprobs = jnp.einsum("bqhd,bkhd->bhqk", dattended, values_in, preferred_element_type=jnp.float32)
    dvalues = jnp.einsum(
        "bhqk,bqhd->bkhd", probs_low, dattended, preferred_element_type=jnp.float32
    )
    dvalues = dvalues.reshape(-1, width).astype(jnp.bfloat16)
    delta = jnp.sum(probs * dprobs, axis=-1, keepdims=True)
    dscores = (probs * (dprobs - delta)).astype(jnp.bfloat16)
    dquery = (
        jnp.einsum("bhqk,bkhd->bqhd", dscores, keys_in, preferred_element_type=jnp.float32) * factor
    )
    dkeys = (
        jnp.einsum("bhqk,bqhd->bkhd", dscores, query, preferred_element_type=jnp.float32) * factor
    )
    dquery = dquery.reshape(-1, width).astype(jnp.bfloat16)
    dkeys = dkeys.reshape(-1, width).astype(jnp.bfloat16)
    dmixed = jnp.concatenate([dquery, dkeys, dvalues], axis=1)
    query_bias_grad = column_sum(dquery)
    value_bias_grad = column_sum(dvalues)
    joint_grad = outer_sum(first_in, dmixed)
    dfirst = back_product(dmixed, joint_back)
    dnorm_one, gain_one_grad, shift_one_grad = norm_back(dfirst, normed_one, inverse_one, gain_one)
    image_grad = (dresid + dnorm_one).reshape(images.shape)
    row_sums = (
        lax.psum_scatter(
            joint_grad.astype(jnp.bfloat16), "fsdp", scatter_dimension=0, tiled=True
        ).astype(jnp.float32),
        lax.psum_scatter(
            out_grad.astype(jnp.bfloat16), "fsdp", scatter_dimension=0, tiled=True
        ).astype(jnp.float32),
        lax.psum_scatter(
            up_grad.astype(jnp.bfloat16), "fsdp", scatter_dimension=0, tiled=True
        ).astype(jnp.float32),
        lax.psum_scatter(
            down_grad.astype(jnp.bfloat16), "fsdp", scatter_dimension=0, tiled=True
        ).astype(jnp.float32),
        lax.psum_scatter(
            gain_one_grad.astype(jnp.bfloat16), "fsdp", scatter_dimension=0, tiled=True
        ).astype(jnp.float32),
        lax.psum_scatter(
            shift_one_grad.astype(jnp.bfloat16), "fsdp", scatter_dimension=0, tiled=True
        ).astype(jnp.float32),
        lax.psum_scatter(
            query_bias_grad.astype(jnp.bfloat16), "fsdp", scatter_dimension=0, tiled=True
        ).astype(jnp.float32),
        lax.psum_scatter(
            value_bias_grad.astype(jnp.bfloat16), "fsdp", scatter_dimension=0, tiled=True
        ).astype(jnp.float32),
        lax.psum_scatter(
            out_bias_grad.astype(jnp.bfloat16), "fsdp", scatter_dimension=0, tiled=True
        ).astype(jnp.float32),
        lax.psum_scatter(
            scale_one_grad.astype(jnp.bfloat16), "fsdp", scatter_dimension=0, tiled=True
        ).astype(jnp.float32),
        lax.psum_scatter(
            gain_two_grad.astype(jnp.bfloat16), "fsdp", scatter_dimension=0, tiled=True
        ).astype(jnp.float32),
        lax.psum_scatter(
            shift_two_grad.astype(jnp.bfloat16), "fsdp", scatter_dimension=0, tiled=True
        ).astype(jnp.float32),
        lax.psum_scatter(
            up_bias_grad.astype(jnp.bfloat16), "fsdp", scatter_dimension=0, tiled=True
        ).astype(jnp.float32),
        lax.psum_scatter(
            down_bias_grad.astype(jnp.bfloat16), "fsdp", scatter_dimension=0, tiled=True
        ).astype(jnp.float32),
        lax.psum_scatter(
            scale_two_grad.astype(jnp.bfloat16), "fsdp", scatter_dimension=0, tiled=True
        ).astype(jnp.float32),
    )
    owned = (
        lax.psum_scatter(
            row_sums[0].astype(jnp.bfloat16), "sub", scatter_dimension=1, tiled=True
        ).astype(jnp.float32),
        lax.psum_scatter(
            row_sums[1].astype(jnp.bfloat16), "sub", scatter_dimension=1, tiled=True
        ).astype(jnp.float32),
        lax.psum_scatter(
            row_sums[2].astype(jnp.bfloat16), "sub", scatter_dimension=1, tiled=True
        ).astype(jnp.float32),
        lax.psum_scatter(
            row_sums[3].astype(jnp.bfloat16), "sub", scatter_dimension=1, tiled=True
        ).astype(jnp.float32),
        lax.psum_scatter(
            row_sums[4].astype(jnp.bfloat16), "sub", scatter_dimension=0, tiled=True
        ).astype(jnp.float32),
        lax.psum_scatter(
            row_sums[5].astype(jnp.bfloat16), "sub", scatter_dimension=0, tiled=True
        ).astype(jnp.float32),
        lax.psum_scatter(
            row_sums[6].astype(jnp.bfloat16), "sub", scatter_dimension=0, tiled=True
        ).astype(jnp.float32),
        lax.psum_scatter(
            row_sums[7].astype(jnp.bfloat16), "sub", scatter_dimension=0, tiled=True
        ).astype(jnp.float32),
        lax.psum_scatter(
            row_sums[8].astype(jnp.bfloat16), "sub", scatter_dimension=0, tiled=True
        ).astype(jnp.float32),
        lax.psum_scatter(
            row_sums[9].astype(jnp.bfloat16), "sub", scatter_dimension=0, tiled=True
        ).astype(jnp.float32),
        lax.psum_scatter(
            row_sums[10].astype(jnp.bfloat16), "sub", scatter_dimension=0, tiled=True
        ).astype(jnp.float32),
        lax.psum_scatter(
            row_sums[11].astype(jnp.bfloat16), "sub", scatter_dimension=0, tiled=True
        ).astype(jnp.float32),
        lax.psum_scatter(
            row_sums[12].astype(jnp.bfloat16), "sub", scatter_dimension=0, tiled=True
        ).astype(jnp.float32),
        lax.psum_scatter(
            row_sums[13].astype(jnp.bfloat16), "sub", scatter_dimension=0, tiled=True
        ).astype(jnp.float32),
        lax.psum_scatter(
            row_sums[14].astype(jnp.bfloat16), "sub", scatter_dimension=0, tiled=True
        ).astype(jnp.float32),
    )
    return (
        block_out,
        image_grad,
        owned[0],
        owned[1],
        owned[2],
        owned[3],
        owned[4],
        owned[5],
        owned[6],
        owned[7],
        owned[8],
        owned[9],
        owned[10],
        owned[11],
        owned[12],
        owned[13],
        owned[14],
    )


def solution(mesh):
    return jax.shard_map(
        shards,
        mesh=mesh,
        in_specs=(
            P(("fsdp", "sub"), None, None),
            P(("fsdp", "sub")),
            P("fsdp", "sub"),
            P("fsdp", "sub"),
            P("fsdp", "sub"),
            P("fsdp", "sub"),
            P(("fsdp", "sub")),
            P(("fsdp", "sub")),
            P(("fsdp", "sub")),
            P(("fsdp", "sub")),
            P(("fsdp", "sub")),
            P(("fsdp", "sub")),
            P(("fsdp", "sub")),
            P(("fsdp", "sub")),
            P(("fsdp", "sub")),
            P(("fsdp", "sub")),
            P(("fsdp", "sub")),
            P(("fsdp", "sub"), None, None),
        ),
        out_specs=(
            P(("fsdp", "sub"), None, None),
            P(("fsdp", "sub"), None, None),
            P("fsdp", "sub"),
            P("fsdp", "sub"),
            P("fsdp", "sub"),
            P("fsdp", "sub"),
            P(("fsdp", "sub")),
            P(("fsdp", "sub")),
            P(("fsdp", "sub")),
            P(("fsdp", "sub")),
            P(("fsdp", "sub")),
            P(("fsdp", "sub")),
            P(("fsdp", "sub")),
            P(("fsdp", "sub")),
            P(("fsdp", "sub")),
            P(("fsdp", "sub")),
            P(("fsdp", "sub")),
        ),
        check_vma=False,
    )
```

profile of v0, /device:TPU:0, one launch (start us, length us, event | category | flops | bytes accessed | tf_op | source)
XLA Modules:
  0.0 791.6 jit_solution(11099384968786636998)
XLA Ops:
  7.4 8.8 %all-gather = bf16[4,576,96]{1,2,0:T(8,128)(2,1)S(1)} all-gather(bf16[1,576,96]{1,2,0:T(8,128)(2,1)} %bitcast.142), channel_id=1, replica_groups=mesh['fsdp'=8,'sub'=4] {'sub'}, dimensions={0}, use_global_device_ids=true | all-gather | bytes 552960 | tf_op jit(solution)/shard_map/all_gather | solution.py:67
  18.6 5.6 all_gather.110
  25.1 8.2 %all_gather.120 = bf16[96,3072]{1,0:T(8,128)(2,1)} all-gather(bf16[96,768]{1,0:T(8,128)(2,1)S(1)} %copy-done.20), channel_id=1, replica_groups=mesh['fsdp'=8,'sub'=4] {'sub'}, dimensions={1}, use_global_device_ids=true | all-gather | bytes 737280 | tf_op jit(solution)/shard_map/all_gather | solution.py:69
  33.4 8.1 %all_gather.124 = bf16[384,768]{0,1:T(8,128)(2,1)} all-gather(bf16[384,192]{0,1:T(8,128)(2,1)S(1)} %copy-done.21), channel_id=1, replica_groups=mesh['fsdp'=8,'sub'=4] {'sub'}, dimensions={1}, use_global_device_ids=true | all-gather | bytes 737280 | tf_op jit(solution)/shard_map/all_gather | solution.py:70
  46.9 6.8 all-reduce.46
  55.8 38.2 %all-reduce.44 = (bf16[768]{0:T(1024)(128)(2,1)S(1)}, bf16[768]{0:T(1024)(128)(2,1)S(1)}, bf16[768]{0:T(1024)(128)(2,1)S(1)}, bf16[768]{0:T(1024)(128)(2,1)S(1)}...) all-reduce(bf16[768]{0:T(1024)(128)(2,1)S(1)} %dynamic-update-slice, ...), channel_id=1, replica_groups=mesh['fsdp'=8,'sub'=4] {'fsdp'}, use_global_device_ids=true, to_apply=%add.5 | all-reduce | flops 7680 | bytes 30720
  95.7 26.3 %all-gather.1 = bf16[8,1,384]{2,1,0:T(2,128)(2,1)S(1)} all-gather(bf16[1,1,384]{2,1,0:T(2,128)(2,1)S(1)} %reshape.257), channel_id=1, replica_groups=mesh['fsdp'=8,'sub'=4] {'fsdp'}, dimensions={0}, use_global_device_ids=true | all-gather | bytes 6912 | tf_op jit(solution)/shard_map/all_gather | solution.py:96
  126.0 6.0 add_convert_fusion
  135.6 2.9 reshape.185
  138.6 3.2 copy.96
  141.8 3.9 reshape.186
  145.6 2.6 copy.94
  148.2 3.9 reshape.184
  152.1 7.8 fusion.56
  159.9 12.6 %fusion.70 = (f32[4,12,256]{2,1,0:T(8,128)S(1)}, f32[4,12,256,256]{2,3,1,0:T(8,128)S(1)}) fusion(f32[4,12,256,256]{2,3,1,0:T(8,128)} %fusion.56, pred[4,256]{1,0:T(4,128)(4,1)S(1)} %get-tuple-element.157), kind=kOutput, calls=%fused_computation.131 | output fusion | flops 18874624 | bytes 25216000 | tf_op jit(solution)/shard_map/sub | solution.py:137
  173.7 3.4 copy-done.6
  178.7 5.2 fusion.66
  186.1 21.9 %all-gather.11.cloned.1.call-done = bf16[768,3072]{1,0:T(8,128)(2,1)} async-done(((bf16[96,3072]{1,0:T(8,128)(2,1)}), bf16[768,3072]{1,0:T(8,128)(2,1)}) %all-gather.11.cloned.1.call-update) | async-done | bytes 4718608 | tf_op jit(solution)/shard_map/all_gather | solution.py:86
  208.0 37.5 %fusion.3 = (bf16[1024,3072]{1,0:T(8,128)(2,1)}, f32[1024,3072]{1,0:T(8,128)}) fusion(f32[3072]{0:T(1024)S(1)} %bitcast.152, bf16[768,3072]{1,0:T(8,128)(2,1)} %all-gather.11.cloned.1.call-done, f32[1024,768]{1,0:T(8,128)} %copy-done.9, f32[768]{0:T(1024)S(1)} %convert_element_type.277, f32[768]{0:T(1024)S(1)} %convert_element_type.276, ...), kind=kOutput, calls=%fused_computation.5 | convolution fusion | flops 5043388416 | bytes 26765312 | tf_op jit(solution)/shard_map/dot_general | solution.py:148
  245.5 43.6 %all-gather.13.cloned.1.call-done = bf16[3072,768]{0,1:T(8,128)(2,1)} async-done(((bf16[384,768]{0,1:T(8,128)(2,1)}), bf16[3072,768]{0,1:T(8,128)(2,1)}) %all-gather.13.cloned.1.call-update) | async-done | bytes 4718608 | tf_op jit(solution)/shard_map/all_gather | solution.py:87
  289.1 12.2 %fusion.73 = (bf16[3072]{0:T(1024)(128)(2,1)S(1)}, bf16[1024,3072]{1,0:T(8,128)(2,1)S(1)}) fusion(f32[1024,3072]{1,0:T(8,128)} %get-tuple-element.162, f32[3072]{0:T(1024)S(1)} %bitcast.153, bf16[1024,768]{1,0:T(8,128)(2,1)S(1)} %copy-done.11, bf16[3072,768]{0,1:T(8,128)(2,1)} %all-gather.13.cloned.1.call-done), kind=kOutput, calls=%fused_computation.134 | convolution fusion | flops 4869583872 | bytes 25184256 | tf_op jit(solution)/shard_map/nb,ab->na/dot_general | solution.py:43
  301.4 7.2 multiply_reduce_fusion.2
  308.7 10.2 %multiply_reduce_fusion.1 = (bf16[768]{0:T(1024)(128)(2,1)S(1)}, bf16[1024,768]{1,0:T(8,128)(2,1)}, bf16[768]{0:T(1024)(128)(2,1)S(1)}, f32[1024,768]{1,0:T(8,128)S(1)}) fusion(bf16[4,256,768]{2,1,0:T(8,128)(2,1)S(1)} %copy-done.8, f32[1024]{0:T(1024)S(1)} %bitcast.151, f32[768]{0:T(1024)S(1)} %copy-done.33, f32[1024,768]{1,0:T(8,128)S(1)} %copy-done.10, ...), kind=kOutput, calls=%fused_computation.59 | convolution fusion | flops 4847564800 | bytes 26774528 | tf_op jit(solution)/shard_map/dot_general | solution.py:150
  321.4 2.4 convolution_convert_fusion.4
  323.8 3.8 convolution_convert_fusion.3
  329.4 2.5 reshape.187
  331.9 12.2 %multiply_reduce_fusion = (f32[4,12,256]{2,1,0:T(8,128)S(1)}, f32[4,12,256,256]{2,3,1,0:T(8,128)}) fusion(f32[4,12,256,256]{2,3,1,0:T(8,128)} %copy-done.6, f32[4,12,256]{2,1,0:T(8,128)S(1)} %get-tuple-element.158, bf16[4,256,12,64]{1,0,3,2:T(4,128)(2,1)} %reshape.184, bf16[4,256,12,64]{1,0,3,2:T(4,128)(2,1)} %reshape.187), kind=kOutput, calls=%fused_computation.13 | convolution fusion | flops 412078080 | bytes 28409856 | tf_op jit(solution)/shard_map/bqhd,bkhd->bhqk/dot_general | solution.py:186
  344.2 9.7 %multiply_convert_fusion = bf16[4,12,256,256]{2,3,1,0:T(8,128)(2,1)S(1)} fusion(f32[4,12,256,256]{2,3,1,0:T(8,128)} %get-tuple-element.165, f32[4,12,256]{2,1,0:T(8,128)S(1)} %get-tuple-element.164, f32[4,12,256,256]{2,3,1,0:T(8,128)} %copy-done.6, f32[4,12,256]{2,1,0:T(8,128)S(1)} %get-tuple-element.158), kind=kLoop, calls=%fused_computation.12 | loop fusion | flops 12582912 | bytes 31555584 | tf_op jit(solution)/shard_map/convert_element_type | solution.py:192
  353.9 6.7 fusion.72
  362.2 2.0 fusion.49
  369.1 2.1 copy-done.19
  371.2 5.6 convolution_convert_fusion.2
  378.3 9.7 %convolution_convert_fusion = bf16[3072,768]{1,0:T(8,128)(2,1)} fusion(bf16[1024,3072]{1,0:T(8,128)(2,1)} %get-tuple-element.161, bf16[1024,768]{1,0:T(8,128)(2,1)S(1)} %copy-done.12), kind=kOutput, calls=%fused_computation.37 | convolution fusion | flops 4834197504 | bytes 12582912 | tf_op jit(solution)/shard_map/na,nb->ab/dot_general | solution.py:39
  388.1 10.5 %convolution_convert_fusion.1 = bf16[768,3072]{1,0:T(8,128)(2,1)} fusion(bf16[1024,3072]{1,0:T(8,128)(2,1)} %copy-done.51, f32[1024,768]{1,0:T(8,128)} %copy-done.9, f32[768]{0:T(1024)S(1)} %convert_element_type.277, f32[768]{0:T(1024)S(1)} %convert_element_type.276, f32[1024]{0:T(1024)S(1)} %add_rsqrt_fusion, f32[1024]{0:T(1024)S(1)} %broadcast_multiply_fusion.4), kind=kOutput, calls=%fused_computation.38 | convolution fusion | flops 4838129664 | bytes 14170112 | tf_op jit(solution)/shard_map/na,nb->ab/dot_general | solution.py:39
  398.7 8.0 %reduce-scatter.17.cloned.1.call-done = bf16[96,768]{1,0:T(8,128)(2,1)} async-done(((bf16[768,768]{1,0:T(8,128)(2,1)}), bf16[96,768]{1,0:T(8,128)(2,1)}) %reduce-scatter.17.cloned.1.call-update) | async-done | bytes 147472 | tf_op jit(solution)/shard_map/reduce_scatter | solution.py:212
  408.5 79.8 %reduce-scatter.15.cloned.1.call-done = bf16[96,2304]{1,0:T(8,128)(2,1)} async-done(((bf16[768,2304]{1,0:T(8,128)(2,1)}), bf16[96,2304]{1,0:T(8,128)(2,1)}) %reduce-scatter.15.cloned.1.call-update) | async-done | bytes 442384 | tf_op jit(solution)/shard_map/reduce_scatter | solution.py:209
  488.3 2.1 copy.121
  493.6 93.4 %reduce-scatter.23.cloned.1.call-done = bf16[384,768]{1,0:T(8,128)(2,1)} async-done(((bf16[3072,768]{1,0:T(8,128)(2,1)}), bf16[384,768]{1,0:T(8,128)(2,1)}) %reduce-scatter.23.cloned.1.call-update) | async-done | bytes 589840 | tf_op jit(solution)/shard_map/reduce_scatter | solution.py:218
  587.0 2.1 copy.125
  589.5 9.5 %fusion.34 = (bf16[768]{0:T(1024)(128)(2,1)S(1)}, f32[1024]{0:T(1024)S(1)}, f32[1024]{0:T(1024)S(1)}, bf16[768]{0:T(1024)(128)(2,1)S(1)}, f32[1024,768]{1,0:T(8,128)}) fusion(bf16[4,256,768]{2,1,0:T(8,128)(2,1)S(1)} %copy-done.1, f32[1024]{0:T(1024)S(1)} %bitcast.145, f32[1024]{0:T(1024)S(1)} %bitcast.148, f32[768]{0:T(1024)S(1)} %copy-done.23, ...), kind=kOutput, calls=%fused_computation.58 | convolution fusion | flops 3631739392 | bytes 12998656 | tf_op jit(solution)/shard_map/nb,ab->na/dot_general | solution.py:43
  599.2 38.0 %all-reduce.43 = (bf16[768]{0:T(1024)(128)(2,1)S(1)}, bf16[768]{0:T(1024)(128)(2,1)S(1)}, bf16[768]{0:T(1024)(128)(2,1)S(1)}, bf16[768]{0:T(1024)(128)(2,1)S(1)}...) all-reduce(bf16[768]{0:T(1024)(128)(2,1)S(1)} %get-tuple-element.87, ...), channel_id=10, replica_groups=mesh['fsdp'=8,'sub'=4] {'fsdp'}, use_global_device_ids=true, to_apply=%region_20.21.clone | all-reduce | flops 10752 | bytes 43008
  638.0 6.1 all-reduce.45
  648.8 37.8 %reduce-scatter.19.cloned.1.call-done = bf16[96,3072]{1,0:T(8,128)(2,1)} async-done(((bf16[768,3072]{1,0:T(8,128)(2,1)}), bf16[96,3072]{1,0:T(8,128)(2,1)}) %reduce-scatter.19.cloned.1.call-update) | async-done | bytes 589840 | tf_op jit(solution)/shard_map/reduce_scatter | solution.py:215
  688.4 4.5 fusion.33
  693.0 16.2 %reduce-scatter.27.cloned.1.call-done = bf16[192,96]{1,0:T(8,128)(2,1)} async-done(((bf16[768,96]{1,0:T(8,128)(2,1)}), bf16[192,96]{1,0:T(8,128)(2,1)}) %reduce-scatter.27.cloned.1.call-update) | async-done | bytes 36880
  710.7 22.9 %reduce-scatter.25.cloned.1.call-done = bf16[576,96]{1,0:T(8,128)(2,1)} async-done(((bf16[2304,96]{1,0:T(8,128)(2,1)}), bf16[576,96]{1,0:T(8,128)(2,1)}) %reduce-scatter.25.cloned.1.call-update) | async-done | bytes 110608
  735.4 22.8 %reduce-scatter.29.cloned.1.call-done = bf16[192,384]{1,0:T(8,128)(2,1)} async-done(((bf16[768,384]{1,0:T(8,128)(2,1)}), bf16[192,384]{1,0:T(8,128)(2,1)}) %reduce-scatter.29.cloned.1.call-update) | async-done | bytes 147472
  760.1 22.6 %reduce-scatter.21.cloned.1.call-done = bf16[96,768]{1,0:T(8,128)(2,1)} async-done(((bf16[96,3072]{1,0:T(8,128)(2,1)}), bf16[96,768]{1,0:T(8,128)(2,1)}) %reduce-scatter.21.cloned.1.call-update) | async-done | bytes 147472 | tf_op jit(solution)/shard_map/reduce_scatter | solution.py:262
  (256 shorter events, 52.1 us)
Async XLA Ops:
  7.2 17.9 %copy-start.20 = (bf16[96,768]{1,0:T(8,128)(2,1)S(1)}, bf16[96,768]{1,0:T(8,128)(2,1)}, u32[]{:S(2)}) copy-start(bf16[96,768]{1,0:T(8,128)(2,1)} %param.22) | copy-start | bytes 442372
  7.2 26.2 %copy-start.21 = (bf16[384,192]{0,1:T(8,128)(2,1)S(1)}, bf16[384,192]{0,1:T(8,128)(2,1)}, u32[]{:S(2)}) copy-start(bf16[384,192]{0,1:T(8,128)(2,1)} %param.23) | copy-start | bytes 442372
  7.2 117.7 %all-gather.7.cloned.1.call-start = ((), (), s32[]{:S(2)}) async-start(), calls=%async_computation.8 | async-start | bytes 3981312 | tf_op jit(solution)/shard_map/all_gather | solution.py:84
  7.3 34.3 %copy-start.34 = (u32[32]{0:T(128)S(1)}, u32[32]{0:T(128)}, u32[]{:S(2)}) copy-start(u32[32]{0:T(128)} %constant.109) | copy-start | bytes 388
  7.3 34.3 %copy-start.35 = (u32[32]{0:T(128)S(1)}, u32[32]{0:T(128)}, u32[]{:S(2)}) copy-start(u32[32]{0:T(128)} %constant.114) | copy-start | bytes 388
  7.3 36.9 %copy-start.39 = (bf16[24]{0:T(256)(128)(2,1)S(1)}, bf16[24]{0:T(256)(128)(2,1)}, u32[]{:S(2)}) copy-start(bf16[24]{0:T(256)(128)(2,1)} %param.29) | copy-start | bytes 148
  7.3 37.1 %copy-start.40 = (bf16[24]{0:T(256)(128)(2,1)S(1)}, bf16[24]{0:T(256)(128)(2,1)}, u32[]{:S(2)}) copy-start(bf16[24]{0:T(256)(128)(2,1)} %param.28) | copy-start | bytes 148
  7.3 37.4 %copy-start.41 = (bf16[24]{0:T(256)(128)(2,1)S(1)}, bf16[24]{0:T(256)(128)(2,1)}, u32[]{:S(2)}) copy-start(bf16[24]{0:T(256)(128)(2,1)} %param.34) | copy-start | bytes 148
  7.3 37.6 %copy-start.42 = (bf16[24]{0:T(256)(128)(2,1)S(1)}, bf16[24]{0:T(256)(128)(2,1)}, u32[]{:S(2)}) copy-start(bf16[24]{0:T(256)(128)(2,1)} %param.30) | copy-start | bytes 148
  7.3 37.9 %copy-start.43 = (bf16[24]{0:T(256)(128)(2,1)S(1)}, bf16[24]{0:T(256)(128)(2,1)}, u32[]{:S(2)}) copy-start(bf16[24]{0:T(256)(128)(2,1)} %param.31) | copy-start | bytes 148
  7.3 38.1 %copy-start.44 = (bf16[24]{0:T(256)(128)(2,1)S(1)}, bf16[24]{0:T(256)(128)(2,1)}, u32[]{:S(2)}) copy-start(bf16[24]{0:T(256)(128)(2,1)} %param.33) | copy-start | bytes 148
  7.3 38.3 %copy-start.45 = (bf16[24]{0:T(256)(128)(2,1)S(1)}, bf16[24]{0:T(256)(128)(2,1)}, u32[]{:S(2)}) copy-start(bf16[24]{0:T(256)(128)(2,1)} %param.24) | copy-start | bytes 148
  7.4 38.6 %copy-start.46 = (bf16[24]{0:T(256)(128)(2,1)S(1)}, bf16[24]{0:T(256)(128)(2,1)}, u32[]{:S(2)}) copy-start(bf16[24]{0:T(256)(128)(2,1)} %param.25) | copy-start | bytes 148
  7.4 38.8 %copy-start.47 = (bf16[24]{0:T(256)(128)(2,1)S(1)}, bf16[24]{0:T(256)(128)(2,1)}, u32[]{:S(2)}) copy-start(bf16[24]{0:T(256)(128)(2,1)} %param.26) | copy-start | bytes 148
  7.4 39.0 %copy-start.48 = (bf16[24]{0:T(256)(128)(2,1)S(1)}, bf16[24]{0:T(256)(128)(2,1)}, u32[]{:S(2)}) copy-start(bf16[24]{0:T(256)(128)(2,1)} %param.27) | copy-start | bytes 148
  7.4 39.3 %copy-start.49 = (bf16[96]{0:T(256)(128)(2,1)S(1)}, bf16[96]{0:T(256)(128)(2,1)}, u32[]{:S(2)}) copy-start(bf16[96]{0:T(256)(128)(2,1)} %param.32) | copy-start | bytes 580
  16.2 77.8 %copy-start = (bf16[4,256,768]{2,1,0:T(8,128)(2,1)S(1)}, bf16[4,256,768]{2,1,0:T(8,128)(2,1)}, u32[]{:S(2)}) copy-start(bf16[4,256,768]{2,1,0:T(8,128)(2,1)} %param.18) | copy-start | bytes 4718596
  17.6 161.1 %all-gather.9.cloned.1.call-start = ((), (), s32[]{:S(2)}) async-start(), calls=%async_computation.9 | async-start | bytes 1327104 | tf_op jit(solution)/shard_map/all_gather | solution.py:85
  25.0 70.0 %copy-start.36 = (s32[4]{0:T(128)S(1)}, s32[4]{0:T(128)}, u32[]{:S(2)}) copy-start(s32[4]{0:T(128)} %param.19) | copy-start | bytes 52
  25.0 97.6 %copy-start.7 = (bf16[4,256,768]{2,1,0:T(8,128)(2,1)S(1)}, bf16[4,256,768]{2,1,0:T(8,128)(2,1)}, u32[]{:S(2)}) copy-start(bf16[4,256,768]{2,1,0:T(8,128)(2,1)} %param.35) | copy-start | bytes 4718596
  25.0 182.9 %all-gather.11.cloned.1.call-start = ((), (), s32[]{:S(2)}) async-start(), calls=%async_computation.10 | async-start | bytes 5308416 | tf_op jit(solution)/shard_map/all_gather | solution.py:86
  33.4 255.7 %all-gather.13.cloned.1.call-start = ((), (), s32[]{:S(2)}) async-start(), calls=%async_computation.11 | async-start | bytes 5308416 | tf_op jit(solution)/shard_map/all_gather | solution.py:87
  41.5 365.2 %reduce-scatter.17.cloned.1.call-start = ((), (), s32[]{:S(2)}) async-start(), calls=%async_computation.13 | async-start | bytes 1327104 | tf_op jit(solution)/shard_map/reduce_scatter | solution.py:212
  94.0 30.2 %copy-start.22 = (f32[768]{0:T(1024)}, f32[768]{0:T(1024)S(1)}, u32[]{:S(2)}) copy-start(f32[768]{0:T(1024)S(1)} %convert_element_type.264) | copy-start | bytes 9220
  94.9 29.3 %copy-start.24 = (f32[1,2,4,128]{3,1,2,0:T(2,128)}, f32[1,2,4,128]{3,1,2,0:T(2,128)S(1)}, u32[]{:S(2)}) copy-start(f32[1,2,4,128]{3,1,2,0:T(2,128)S(1)} %copy.128) | copy-start | bytes 12292
  94.9 29.3 %copy-start.26 = (f32[1,2,4,128]{3,1,2,0:T(2,128)}, f32[1,2,4,128]{3,1,2,0:T(2,128)S(1)}, u32[]{:S(2)}) copy-start(f32[1,2,4,128]{3,1,2,0:T(2,128)S(1)} %copy.127) | copy-start | bytes 12292
  138.6 13.5 %copy-start.2 = (bf16[4,256,12,64]{1,0,3,2:T(4,128)(2,1)}, bf16[4,256,12,64]{1,0,3,2:T(4,128)(2,1)S(1)}, u32[]{:S(2)}) copy-start(bf16[4,256,12,64]{1,0,3,2:T(4,128)(2,1)S(1)} %reshape.185) | copy-start | bytes 4718596
  159.9 12.7 %copy-start.15 = (bf16[4,256,12,64]{1,0,3,2:T(4,128)(2,1)S(1)}, bf16[4,256,12,64]{1,0,3,2:T(4,128)(2,1)}, u32[]{:S(2)}) copy-start(bf16[4,256,12,64]{1,0,3,2:T(4,128)(2,1)} %reshape.184) | copy-start | bytes 4718596
  208.0 81.1 %copy-start.11 = (bf16[1024,768]{1,0:T(8,128)(2,1)S(1)}, bf16[1024,768]{1,0:T(8,128)(2,1)}, u32[]{:S(2)}) copy-start(bf16[1024,768]{1,0:T(8,128)(2,1)} %multiply_convert_fusion.5) | copy-start | bytes 4718596
  289.1 12.2 %copy-start.10 = (f32[1024,768]{1,0:T(8,128)S(1)}, f32[1024,768]{1,0:T(8,128)}, u32[]{:S(2)}) copy-start(f32[1024,768]{1,0:T(8,128)} %copy-done.9) | copy-start | bytes 9437188
  289.1 12.2 %copy-start.38 = (bf16[768,3072]{1,0:T(8,128)(2,1)S(1)}, bf16[768,3072]{1,0:T(8,128)(2,1)}, u32[]{:S(2)}) copy-start(bf16[768,3072]{1,0:T(8,128)(2,1)} %all-gather.11.cloned.1.call-done) | copy-start | bytes 14155780
  301.3 7.3 copy-start.51
  301.3 7.3 copy-start.8
  301.3 7.3 copy-start.29
  301.4 7.3 copy-start.32
  344.1 144.2 %reduce-scatter.15.cloned.1.call-start = ((), (), s32[]{:S(2)}) async-start(), calls=%async_computation.12 | async-start | bytes 3981312 | tf_op jit(solution)/shard_map/reduce_scatter | solution.py:209
  344.2 9.7 %copy-start.18 = (bf16[4,256,12,64]{1,0,3,2:T(4,128)(2,1)S(1)}, bf16[4,256,12,64]{1,0,3,2:T(4,128)(2,1)}, u32[]{:S(2)}) copy-start(bf16[4,256,12,64]{1,0,3,2:T(4,128)(2,1)} %reshape.187) | copy-start | bytes 4718596
  376.9 210.1 %reduce-scatter.23.cloned.1.call-start = ((), (), s32[]{:S(2)}) async-start(), calls=%async_computation.16 | async-start | bytes 5308416 | tf_op jit(solution)/shard_map/reduce_scatter | solution.py:218
  388.0 298.6 %reduce-scatter.19.cloned.1.call-start = ((), (), s32[]{:S(2)}) async-start(), calls=%async_computation.14 | async-start | bytes 5308416 | tf_op jit(solution)/shard_map/reduce_scatter | solution.py:215
  398.6 94.5 %copy-start.30 = (f32[4,256]{1,0:T(4,128)S(1)}, f32[4,256]{1,0:T(4,128)}, u32[]{:S(2)}) copy-start(f32[4,256]{1,0:T(4,128)} %get-tuple-element.155) | copy-start | bytes 12292
  398.6 190.8 %copy-start.1 = (bf16[4,256,768]{2,1,0:T(8,128)(2,1)S(1)}, bf16[4,256,768]{2,1,0:T(8,128)(2,1)}, u32[]{:S(2)}) copy-start(bf16[4,256,768]{2,1,0:T(8,128)(2,1)} %param.18) | copy-start | bytes 4718596
  398.6 190.8 %copy-start.23 = (f32[768]{0:T(1024)S(1)}, f32[768]{0:T(1024)}, u32[]{:S(2)}) copy-start(f32[768]{0:T(1024)} %copy-done.22) | copy-start | bytes 9220
  398.6 190.8 %copy-start.25 = (f32[1,2,4,128]{3,1,2,0:T(2,128)S(1)}, f32[1,2,4,128]{3,1,2,0:T(2,128)}, u32[]{:S(2)}) copy-start(f32[1,2,4,128]{3,1,2,0:T(2,128)} %copy-done.24) | copy-start | bytes 12292
  398.7 190.8 %copy-start.27 = (f32[1,2,4,128]{3,1,2,0:T(2,128)S(1)}, f32[1,2,4,128]{3,1,2,0:T(2,128)}, u32[]{:S(2)}) copy-start(f32[1,2,4,128]{3,1,2,0:T(2,128)} %copy-done.26) | copy-start | bytes 12292
  398.7 310.5 %reduce-scatter.27.cloned.1.call-start = ((), (), s32[]{:S(2)}) async-start(), calls=%async_computation.18 | async-start | bytes 245760
  408.5 325.2 %reduce-scatter.25.cloned.1.call-start = ((), (), s32[]{:S(2)}) async-start(), calls=%async_computation.17 | async-start | bytes 737280
  490.5 267.7 %reduce-scatter.29.cloned.1.call-start = ((), (), s32[]{:S(2)}) async-start(), calls=%async_computation.19 | async-start | bytes 737280
  589.1 193.5 %reduce-scatter.21.cloned.1.call-start = ((), (), s32[]{:S(2)}) async-start(), calls=%async_computation.15 | async-start | bytes 737280 | tf_op jit(solution)/shard_map/reduce_scatter | solution.py:262
  (16 other events, 52.9 us)
Sparse Core Ops, SparseCore 0:
  17.8 66.8 all-gather.6
  87.4 39.6 all-gather.8
  129.3 78.6 all-gather.10
  209.9 79.1 all-gather.12
  344.3 62.4 reduce-scatter.16
  410.2 78.1 reduce-scatter.14
  492.0 94.9 reduce-scatter.22
  590.6 95.9 reduce-scatter.18
  689.7 19.4 reduce-scatter.26
  711.5 22.0 reduce-scatter.24
  736.1 22.0 reduce-scatter.28
  760.6 22.0 reduce-scatter.20
where the time goes:
time: 799 us; the launch traced here: 792 us
  waiting for transfers between devices  369 us (46%)
  matrix products  151 us (19%)
  blocking collectives  146 us (18%)
  local copies, waits for them, and re-layouts  62 us (8%)
  other arithmetic  42.2 us (5%)
  between operations  20.1 us (3%)
    reduce_scatter x1, waiting for transfers between devices, shards(): lax.psum_scatter(down_grad.astype(jnp.bfloat16), 'fsdp', scatter_dimensio...  93.4 us
    unnamed x4, blocking collectives  89.1 us
    reduce_scatter x1, waiting for transfers between devices, shards(): lax.psum_scatter(joint_grad.astype(jnp.bfloat16), 'fsdp', scatter_dimensi...  79.8 us
    unnamed x15, waiting for transfers between devices  62.1 us
    all_gather x1, waiting for transfers between devices, shards(): lax.all_gather(columns[3], 'fsdp', axis=0, tiled=True)  43.6 us
    reduce_scatter x1, waiting for transfers between devices, shards(): lax.psum_scatter(up_grad.astype(jnp.bfloat16), 'fsdp', scatter_dimension=...  37.8 us
    dot_general x1, matrix products, shards(): jnp.dot(second_in, up_full, preferred_element_type=jnp.float32) + up_add  37.5 us
    dot_general x4, matrix products, back_product(): jnp.einsum('nb,ab->na', left, weight, preferred_element_type=jnp.float32)  32.8 us
  transfers between devices with their start and end apart: 12, of which 10 were waited for; matrix products, arithmetic and copies ran while one was open for 24% of the time, Pallas kernels for 0%

commit v1 on v0

v1 whole, which is shorter than its diff:
```python
import functools
import math

import jax
import jax.numpy as jnp
from jax import lax
from jax.experimental import pallas as pl
from jax.experimental.pallas import tpu as pltpu
from jax.sharding import PartitionSpec as P

HD = 64
EPS = 1e-06
NEGATIVE = -1e30
ROW_TILES = 8
COL_TILES = 4
PIECES = ROW_TILES * COL_TILES
HALF = PIECES // 2
PARTS = 3
BOTH = ("fsdp", "sub")
VMEM_LIMIT = 56 * 1024 * 1024
BF = jnp.bfloat16
F32 = jnp.float32
NT = (((1,), (1,)), ((), ()))
TN = (((0,), (0,)), ((), ()))


def dot(left, right):
    return jnp.dot(left, right, preferred_element_type=F32)


def dot_general(left, right, dims):
    return lax.dot_general(left, right, dims, preferred_element_type=F32)


def normalize(rows):
    centre = rows - jnp.mean(rows, axis=-1, keepdims=True)
    spread = jnp.mean(centre * centre, axis=-1, keepdims=True)
    inverse = lax.rsqrt(spread + EPS)
    return (centre * inverse, inverse)


def norm_back(upstream, normed, inverse, gain):
    scaled = upstream * gain
    return inverse * (
        scaled
        - jnp.mean(scaled, axis=-1, keepdims=True)
        - normed * jnp.mean(scaled * normed, axis=-1, keepdims=True)
    )


def row_sum(values):
    return jnp.sum(values, axis=0, keepdims=True)


def whole(shape):
    zeros = (0,) * len(shape)
    return pl.BlockSpec(shape, lambda *_: zeros, pipeline_mode=pl.Buffered(1))


def whole_out(shape):
    zeros = (0,) * len(shape)
    return pl.BlockSpec(shape, lambda *_: zeros)


ANY = pl.BlockSpec(memory_space=pl.ANY)


def params():
    return pltpu.CompilerParams(
        dimension_semantics=("arbitrary",), vmem_limit_bytes=VMEM_LIMIT
    )


def cost(flops, moved, trans=0):
    return pl.CostEstimate(flops=flops, bytes_accessed=moved, transcendentals=trans)


def stage_joint(dest, own, other, weights, sems):
    copies = []
    for i in range(PIECES):
        place = dest[i]
        source = own.at[i] if i < HALF else other.at[i - HALF]
        copies.append(
            pltpu.make_async_copy(
                source,
                weights.at[lax.rem(place, COL_TILES), lax.div(place, COL_TILES)],
                sems.at[i],
            )
        )
    for copy in copies:
        copy.start()
    for copy in copies:
        copy.wait()


def joint_columns(weights, s, width):
    return weights[s].reshape(width, width)


def qkv_kernel(dest, images, table, bias, own, other, mixed, first_t, weights, sems):
    width = images.shape[-1]
    span = 3 * width // COL_TILES

    @pl.when(pl.program_id(0) == 0)
    def _():
        stage_joint(dest, own, other, weights, sems)

    normed, _ = normalize(images[0].astype(F32))
    first = (normed * table[0:1] + table[1:2]).astype(BF)
    first_t[...] = first.T
    for s in range(COL_TILES):
        out = dot(first, joint_columns(weights, s, width))
        out = (out + bias[s : s + 1]).astype(BF)
        mixed[s * span : (s + 1) * span, :] = out.T[:span]


def attention_kernel(counts, mixed, attended, probs):
    width = attended.shape[0]
    length = mixed.shape[1]
    scale = math.log2(math.e) / math.sqrt(HD)
    count = counts[pl.program_id(0)]
    valid = lax.broadcasted_iota(jnp.int32, (length, length), 0) < count
    for h in range(width // HD):
        query = mixed[h * HD : (h + 1) * HD, :]
        key = mixed[width + h * HD : width + (h + 1) * HD, :]
        value = mixed[2 * width + h * HD : 2 * width + (h + 1) * HD, :]
        scores = jnp.where(valid, dot_general(key, query, TN), NEGATIVE)
        largest = jnp.max(scores, axis=0, keepdims=True)
        expon = jnp.exp2((scores - largest) * scale)
        low = (expon * (1.0 / jnp.sum(expon, axis=0, keepdims=True))).astype(BF)
        probs[0, h] = low
        attended[h * HD : (h + 1) * HD, :] = dot(value, low).astype(BF)


def second_kernel(
    dest,
    counts,
    images,
    cotangent,
    attended,
    table,
    own,
    other,
    resid_out,
    branch_out,
    second,
    second_t,
    dfeed_out,
    dfeed_t,
    out_full,
    weights,
    sems,
):
    width = images.shape[-1]
    length = images.shape[1]
    span = 3 * width // COL_TILES
    piece = width // COL_TILES

    @pl.when(pl.program_id(0) == 0)
    def _():
        stage_joint(dest, own, other, weights, sems)
        for s in range(COL_TILES):
            out_full[:, s * piece : (s + 1) * piece] = joint_columns(weights, s, width)[:, span:]

    branch = dot_general(attended[...], out_full[...], TN) + table[4:5]
    branch_out[...] = branch.astype(BF)
    resid = images[0].astype(F32) + table[5:6] * branch
    resid_out[...] = resid
    normed, _ = normalize(resid)
    second_in = (normed * table[6:7] + table[7:8]).astype(BF)
    second[...] = second_in
    second_t[...] = second_in.T
    rows = lax.broadcasted_iota(jnp.int32, (length, 1), 0)
    mask = (rows < counts[pl.program_id(0)]).astype(F32)
    dfeed = (cotangent[0].astype(F32) * mask * table[9:10]).astype(BF)
    dfeed_out[...] = dfeed
    dfeed_t[...] = dfeed.T


def gelu_pair(value):
    size = jnp.abs(value)
    t = 1.0 / (1.0 + (0.3275911 / math.sqrt(2.0)) * size)
    bell = jnp.exp2(value * value * (-0.5 * math.log2(math.e)))
    poly = 0.5 * 1.061405429
    for c in (-1.453152027, 1.421413741, -0.284496736, 0.254829592):
        poly = poly * t + 0.5 * c
    tail = poly * t * bell
    cumul = jnp.where(value >= 0, 1.0 - tail, tail)
    return value * cumul, cumul + value * bell * (1.0 / math.sqrt(2.0 * math.pi))


def mlp_kernel(
    first,
    group,
    base,
    dest,
    second,
    second_t,
    dfeed,
    dfeed_t,
    bias,
    own,
    other,
    *rest,
):
    if not first:
        feed_in, dsecond_in, rest = rest[0], rest[1], rest[2:]
    feed, dsecond, bias_grad, keep, send, up, down, up_grad, down_grad, sems = rest
    width = second.shape[1]
    depth = width // ROW_TILES
    span = width // COL_TILES
    lane = up.shape[-1] // 2
    step = pl.program_id(0)
    steps = pl.num_programs(0)
    tile = 256

    def pairs(i):
        place = dest[i]
        m = lax.div(place, COL_TILES)
        s = lax.rem(place, COL_TILES)
        rows = pl.multiple_of(m * depth, 16)
        out = []
        for g in range(group):
            out.append((g, s, rows, depth, 0, 2 * lane, True))
            for h in range(2):
                low = pl.multiple_of(s * span + h * depth, 16)
                out.append((g, m, low, depth, h * lane, lane, False))
        return out

    def move(i, buffer_up, buffer_down, outside, origin, inward):
        copies = []
        for n, (g, q, rows, count, at, wide, is_up) in enumerate(pairs(i)):
            top = origin + g * 2 * depth + (0 if is_up else depth)
            far = outside.at[i % HALF, pl.ds(top, count), pl.ds(at, wide)]
            if is_up:
                near = buffer_up.at[g * COL_TILES + q, pl.ds(rows, count), :]
            else:
                near = buffer_down.at[
                    g * COL_TILES + lax.div(q, 2),
                    pl.ds(rows, count),
                    pl.ds(pl.multiple_of(lax.rem(q, 2) * lane, 128), lane),
                ]
            pair = (far, near) if inward else (near, far)
            copies.append(pltpu.make_async_copy(*pair, sems.at[i]))
        return copies

    @pl.when(step == 0)
    def _():
        copies = []
        for i in range(PIECES):
            copies += move(i, up, down, own if i < HALF else other, base, True)
        for copy in copies:
            copy.start()
        if first:
            feed[...] = jnp.zeros(feed.shape, F32)
            dsecond[...] = jnp.zeros(dsecond.shape, F32)
        else:
            feed[...] = feed_in[...]
            dsecond[...] = dsecond_in[...]
        for copy in copies:
            copy.wait()

    up_now = up[step]
    down_now = down[step]
    hiddens = []
    dpres = []
    total = jnp.zeros((1, 2 * lane), F32)
    for r in range(second.shape[0] // tile):
        rows = slice(r * tile, (r + 1) * tile)
        pre = dot(second[rows, :], up_now) + bias[pl.ds(step, 1), :]
        dhidden = dot(dfeed[rows, :], down_now)
        hidden, slope = gelu_pair(pre)
        hidden = hidden.astype(BF)
        dpre = (dhidden * slope).astype(BF)
        total = total + row_sum(dpre.astype(F32))
        feed[rows, :] += dot_general(hidden, down_now, NT)
        dsecond[rows, :] += dot_general(dpre, up_now, NT)
        hiddens.append(hidden)
        dpres.append(dpre)
    bias_grad[pl.ds(step, 1), :] = total
    up_grad[step] = dot(second_t[...], jnp.concatenate(dpres, axis=0)).astype(BF)
    down_grad[step] = dot(dfeed_t[...], jnp.concatenate(hiddens, axis=0)).astype(BF)

    @pl.when(step == steps - 1)
    def _():
        copies = []
        for i in range(PIECES):
            copies += move(i, up_grad, down_grad, keep if i < HALF else send, 0, False)
        for copy in copies:
            copy.start()
        for copy in copies:
            copy.wait()


def middle_kernel(
    counts,
    cotangent,
    feed,
    dsecond,
    resid,
    branch,
    attended,
    out_full,
    table,
    block_out,
    dresid_out,
    dattended,
    out_grad,
    sums,
    total,
):
    length = cotangent.shape[1]
    step = pl.program_id(0)

    @pl.when(step == 0)
    def _():
        total[...] = jnp.zeros(total.shape, F32)
        sums[...] = jnp.zeros(sums.shape, F32)

    rows = lax.broadcasted_iota(jnp.int32, (length, 1), 0)
    mask = (rows < counts[step]).astype(F32)
    feed_out = feed[...] + table[8:9]
    grad = cotangent[0].astype(F32) * mask
    value = resid[...]
    block_out[0] = ((value + table[9:10] * feed_out) * mask).astype(BF)
    normed, inverse = normalize(value)
    upstream = dsecond[...]
    dresid = grad + norm_back(upstream, normed, inverse, table[6:7])
    dresid_out[...] = dresid
    dbranch = (dresid * table[5:6]).astype(BF)
    dfeed = (grad * table[9:10]).astype(BF)
    sums[0:1] += row_sum(dbranch.astype(F32))
    sums[1:2] += row_sum(dresid * branch[...].astype(F32))
    sums[2:3] += row_sum(upstream * normed)
    sums[3:4] += row_sum(upstream)
    sums[4:5] += row_sum(dfeed.astype(F32))
    sums[5:6] += row_sum(grad * feed_out)
    total[...] += dot(attended[...], dbranch)
    dattended[...] = dot_general(out_full[...], dbranch, NT).astype(BF)

    @pl.when(step == pl.num_programs(0) - 1)
    def _():
        out_grad[...] = total[...].astype(BF)


def attention_back_kernel(mixed, probs, attended, dattended, dmixed, sums, dquery_sum, dvalue_sum):
    width = attended.shape[0]
    length = mixed.shape[1]
    factor = 1.0 / math.sqrt(HD)
    step = pl.program_id(0)

    @pl.when(step == 0)
    def _():
        dquery_sum[...] = jnp.zeros(dquery_sum.shape, F32)
        dvalue_sum[...] = jnp.zeros(dvalue_sum.shape, F32)

    def fold(values):
        values = values.astype(F32)
        return sum(values[:, a : a + 128] for a in range(0, length, 128))

    for h in range(width // HD):
        at = slice(h * HD, (h + 1) * HD)
        query = mixed[h * HD : (h + 1) * HD, :]
        key = mixed[width + h * HD : width + (h + 1) * HD, :]
        value = mixed[2 * width + h * HD : 2 * width + (h + 1) * HD, :]
        upstream = dattended[at, :]
        low = probs[0, h]
        delta = row_sum(upstream.astype(F32) * attended[at, :].astype(F32))
        dprobs = dot_general(value, upstream, TN)
        dscores = (low.astype(F32) * (dprobs - delta)).astype(BF)
        dvalue = dot_general(upstream, low, NT).astype(BF)
        dkey = (dot_general(query, dscores, NT) * factor).astype(BF)
        dquery = (dot(key, dscores) * factor).astype(BF)
        dmixed[at, :] = dquery
        dmixed[width + h * HD : width + (h + 1) * HD, :] = dkey
        dmixed[2 * width + h * HD : 2 * width + (h + 1) * HD, :] = dvalue
        dquery_sum[at, :] += fold(dquery)
        dvalue_sum[at, :] += fold(dvalue)

    @pl.when(step == pl.num_programs(0) - 1)
    def _():
        sums[...] = jnp.zeros(sums.shape, F32)
        sums[0:1] = row_sum(dquery_sum[...].T)
        sums[1:2] = row_sum(dvalue_sum[...].T)


def joint_grad_kernel(dest, first_t, dmixed, out_grad, keep, send, grads, sems):
    width = first_t.shape[0]
    depth = width // ROW_TILES
    span = dmixed.shape[0]
    piece = width // COL_TILES
    step = pl.program_id(0)
    grads[step, :, 0:span] = dot_general(first_t[...], dmixed[...], NT).astype(BF)

    @pl.when(step == pl.num_programs(0) - 1)
    def _():
        for s in range(COL_TILES):
            grads[s, :, span:] = out_grad[:, s * piece : (s + 1) * piece]
        copies = []
        for i in range(PIECES):
            place = dest[i]
            m = lax.div(place, COL_TILES)
            near = grads.at[
                lax.rem(place, COL_TILES), pl.ds(pl.multiple_of(m * depth, 16), depth), :
            ]
            far = keep.at[i] if i < HALF else send.at[i - HALF]
            copies.append(pltpu.make_async_copy(near, far, sems.at[i]))
        for copy in copies:
            copy.start()
        for copy in copies:
            copy.wait()


def input_grad_kernel(
    dest, images, dresid, dmixed, table, own, other, image_grad, sums, weights, sems
):
    width = images.shape[-1]
    span = 3 * width // COL_TILES

    @pl.when(pl.program_id(0) == 0)
    def _():
        stage_joint(dest, own, other, weights, sems)
        sums[...] = jnp.zeros(sums.shape, F32)

    back = None
    for s in range(COL_TILES):
        part = dot(
            joint_columns(weights, s, width)[:, :span], dmixed[s * span : (s + 1) * span, :]
        )
        back = part if back is None else back + part
    upstream = back.T
    normed, inverse = normalize(images[0].astype(F32))
    sums[0:1] += row_sum(upstream * normed)
    sums[1:2] += row_sum(upstream)
    image_grad[0] = dresid[...] + norm_back(upstream, normed, inverse, table[0:1])


def flat_pairs(fsdp, sub, there):
    return [(f * sub + s, there(f, s)) for f in range(fsdp) for s in range(sub)]


class Cube:
    def __init__(self):
        def along_z(k):
            return flat_pairs(8, 4, lambda f, s: (f ^ (2 * k)) * 4 + s)

        def y_or_x(order):
            def there(f, s):
                turn = (s % 2) ^ order
                return (f * 4 + (s ^ 2)) if turn else ((f ^ 1) * 4 + s)

            return flat_pairs(8, 4, there)

        self.z = [along_z(k) for k in (1, 2, 3)]
        self.plane = [y_or_x(0), y_or_x(1)]
        self.core = flat_pairs(8, 4, lambda f, s: f * 4 + (s ^ 1))
        self.y = flat_pairs(8, 4, lambda f, s: (f ^ 1) * 4 + s)
        self.x = flat_pairs(8, 4, lambda f, s: f * 4 + (s ^ 2))

    def swap(self, value, pairs):
        return lax.ppermute(value, BOTH, pairs)

    def places(self):
        f = lax.axis_index("fsdp")
        s = lax.axis_index("sub")
        z, y, x, c = f // 2, f % 2, s // 2, s % 2

        def slot_to_place(i):
            core = c ^ (i // 16)
            far, near, dz = (i // 8) % 2, (i // 4) % 2, i % 4
            dy = jnp.where(core == 0, near, far)
            dx = jnp.where(core == 0, far, near)
            return ((z ^ dz) * 2 + (y ^ dy)) * 4 + (x ^ dx) * 2 + core

        def place_to_slot(p):
            pf, ps = p // 4, p % 4
            core = ps % 2
            dz, dy, dx = z ^ (pf // 2), y ^ (pf % 2), x ^ (ps // 2)
            near = jnp.where(core == 0, dy, dx)
            far = jnp.where(core == 0, dx, dy)
            return (c ^ core) * 16 + far * 8 + near * 4 + dz

        index = jnp.arange(PIECES, dtype=jnp.int32)
        return slot_to_place(index), place_to_slot(index)

    def gather(self, piece):
        four = jnp.stack([piece] + [self.swap(piece, pairs) for pairs in self.z])
        eight = jnp.concatenate([four, self.swap(four, self.plane[0])])
        own = jnp.concatenate([eight, self.swap(eight, self.plane[1])])
        return own, self.swap(own, self.core)

    def reduce(self, keep, send):
        def add(*terms):
            return sum(term.astype(F32) for term in terms).astype(BF)

        got = self.swap(send, self.core)
        low, high = add(keep[:8], got[:8]), add(keep[8:], got[8:])
        got = self.swap(high, self.plane[1])
        low, high = add(low[:4], got[:4]), add(low[4:], got[4:])
        got = self.swap(high, self.plane[0])
        four = [add(low[k], got[k]) for k in range(4)]
        total = four[0].astype(F32)
        for k in (1, 2, 3):
            total = total + self.swap(four[k], self.z[k - 1]).astype(F32)
        return total

    def total(self, value):
        for pairs in (self.core, self.x, self.y, self.z[0], self.z[1]):
            value = value + self.swap(value, pairs)
        return value


def gather_vectors(cube, slot_of, vectors):
    short = vectors[0].shape[0]
    if cube is None:
        full = [lax.all_gather(v, BOTH, axis=0, tiled=True).astype(F32) for v in vectors]
        return full
    flat = jnp.concatenate(vectors)
    piece = jnp.pad(flat, (0, 1024 - flat.shape[0])).reshape(8, 128)
    own, other = cube.gather(piece)
    every = jnp.concatenate([own, other]).reshape(PIECES, 1024)
    pick = (slot_of[:, None] == jnp.arange(PIECES)[None, :]).astype(BF)
    every = dot(pick, every)
    full = []
    at = 0
    for vector in vectors:
        full.append(every[:, at : at + vector.shape[0]].reshape(-1))
        at += vector.shape[0]
    return full


def shards(
    images,
    counts,
    joint_weight,
    out_weight,
    up_weight,
    down_weight,
    first_gain,
    first_shift,
    query_bias,
    value_bias,
    out_bias,
    first_scale,
    second_gain,
    second_shift,
    up_bias,
    down_bias,
    second_scale,
    cotangent,
    sizes,
):
    fsdp, sub = sizes
    cube = Cube() if (fsdp, sub) == (8, 4) else None
    images_here, length, width = images.shape
    heads = width // HD
    rows = images_here * length
    hidden_units = up_weight.shape[1] * sub
    depth = width // ROW_TILES
    span = 3 * width // COL_TILES
    piece = width // COL_TILES
    part = hidden_units // PARTS
    lane = part // ROW_TILES
    steps = COL_TILES

    if cube is not None:
        dest, slot_of = cube.places()
        first_piece = jnp.concatenate([joint_weight, out_weight], axis=1)
        up_parts = up_weight.reshape(depth, 2, PARTS, lane)
        down_parts = down_weight.T.reshape(2, depth, PARTS, lane)
        feed_piece = jnp.concatenate(
            [
                jnp.concatenate(
                    [
                        up_parts[:, :, j].reshape(depth, 2 * lane),
                        down_parts[:, :, j].transpose(1, 0, 2).reshape(depth, 2 * lane),
                    ]
                )
                for j in range(PARTS)
            ]
        )
        own_first, other_first = cube.gather(first_piece)
        own_feed, other_feed = cube.gather(feed_piece)
    else:
        dest = jnp.arange(PIECES, dtype=jnp.int32)
        slot_of = dest

        def fetch(value):
            return lax.all_gather(
                lax.all_gather(value, "sub", axis=1, tiled=True), "fsdp", axis=0, tiled=True
            )

        def cut(value, columns):
            value = value.reshape(ROW_TILES, depth, COL_TILES, columns)
            return value.transpose(0, 2, 1, 3).reshape(PIECES, depth, columns)

        first_pieces = jnp.concatenate(
            [cut(fetch(joint_weight), span), cut(fetch(out_weight), piece)], axis=2
        )
        up_parts = fetch(up_weight).reshape(ROW_TILES, depth, COL_TILES, 2, PARTS, lane)
        up_parts = up_parts.transpose(0, 2, 4, 1, 3, 5)
        down_parts = fetch(down_weight).reshape(ROW_TILES, PARTS, lane, COL_TILES, 2, depth)
        down_parts = down_parts.transpose(0, 3, 1, 5, 4, 2)
        shape = (PIECES, PARTS, depth, 2 * lane)
        feed_pieces = jnp.concatenate(
            [up_parts.reshape(shape), down_parts.reshape(shape)], axis=2
        ).reshape(PIECES, PARTS * 2 * depth, 2 * lane)
        own_first, other_first = first_pieces[:HALF], first_pieces[HALF:]
        own_feed, other_feed = feed_pieces[:HALF], feed_pieces[HALF:]

    (
        gain_one,
        shift_one,
        query_add,
        value_add,
        out_add,
        scale_one,
        gain_two,
        shift_two,
        up_add,
        down_add,
        scale_two,
    ) = gather_vectors(
        cube,
        slot_of,
        (
            first_gain,
            first_shift,
            query_bias,
            value_bias,
            out_bias,
            first_scale,
            second_gain,
            second_shift,
            up_bias,
            down_bias,
            second_scale,
        ),
    )
    table = jnp.stack(
        [
            gain_one,
            shift_one,
            query_add,
            value_add,
            out_add,
            scale_one,
            gain_two,
            shift_two,
            down_add,
            scale_two,
        ]
    )
    joint_bias = jnp.concatenate([query_add, jnp.zeros_like(query_add), value_add])
    joint_bias = jnp.pad(joint_bias.reshape(COL_TILES, span), ((0, 0), (0, piece)))
    up_rows = up_add.reshape(ROW_TILES, PARTS, lane).transpose(1, 0, 2)
    up_rows = up_rows.reshape(PARTS, steps, 2 * lane)

    def sds(shape, dtype):
        return jax.ShapeDtypeStruct(shape, dtype)

    image_block = pl.BlockSpec((1, length, width), lambda i, *_: (i, 0, 0))
    row_block = pl.BlockSpec((length, width), lambda i, *_: (i, 0))
    column_block = pl.BlockSpec((width, length), lambda i, *_: (0, i))
    mixed_block = pl.BlockSpec((3 * width, length), lambda i, *_: (0, i))
    probs_block = pl.BlockSpec((1, heads, length, length), lambda i, *_: (i, 0, 0, 0))
    table_spec = whole(table.shape)
    joint_scratch = [
        pltpu.VMEM((COL_TILES, ROW_TILES, depth, width), BF),
        pltpu.SemaphoreType.DMA((PIECES,)),
    ]

    mixed, first_t = pl.pallas_call(
        qkv_kernel,
        grid_spec=pltpu.PrefetchScalarGridSpec(
            num_scalar_prefetch=1,
            grid=(images_here,),
            in_specs=[image_block, table_spec, whole(joint_bias.shape), ANY, ANY],
            out_specs=[mixed_block, column_block],
            scratch_shapes=joint_scratch,
        ),
        out_shape=[sds((3 * width, rows), BF), sds((width, rows), BF)],
        compiler_params=params(),
        cost_estimate=cost(2 * rows * width * 3 * width, 14 * rows * width),
        name="qkv",
    )(dest, images, table, joint_bias, own_first, other_first)

    attended, probs = pl.pallas_call(
        attention_kernel,
        grid_spec=pltpu.PrefetchScalarGridSpec(
            num_scalar_prefetch=1,
            grid=(images_here,),
            in_specs=[mixed_block],
            out_specs=[column_block, probs_block],
        ),
        out_shape=[
            sds((width, rows), BF),
            sds((images_here, heads, length, length), BF),
        ],
        compiler_params=params(),
        cost_estimate=cost(16 * rows * width * length, 8 * rows * width),
        name="attention",
    )(counts, mixed)

    resid, branch, second, second_t, dfeed, dfeed_t, out_full = pl.pallas_call(
        second_kernel,
        grid_spec=pltpu.PrefetchScalarGridSpec(
            num_scalar_prefetch=2,
            grid=(images_here,),
            in_specs=[image_block, image_block, column_block, table_spec, ANY, ANY],
            out_specs=[
                row_block,
                row_block,
                row_block,
                column_block,
                row_block,
                column_block,
                whole_out((width, width)),
            ],
            scratch_shapes=joint_scratch,
        ),
        out_shape=[
            sds((rows, width), F32),
            sds((rows, width), BF),
            sds((rows, width), BF),
            sds((width, rows), BF),
            sds((rows, width), BF),
            sds((width, rows), BF),
            sds((width, width), BF),
        ],
        compiler_params=params(),
        cost_estimate=cost(2 * rows * width * width, 20 * rows * width),
        name="second_norm",
    )(dest, counts, images, cotangent, attended, table, own_first, other_first)

    feed = dsecond = None
    up_sums = []
    feed_grads = []
    square = (rows, width)
    for j in range(PARTS):
        start = j == 0
        extra = [] if start else [feed, dsecond]
        feed, dsecond, bias_sum, keep, send = pl.pallas_call(
            functools.partial(mlp_kernel, start, 1, j * 2 * depth),
            grid_spec=pltpu.PrefetchScalarGridSpec(
                num_scalar_prefetch=1,
                grid=(steps,),
                in_specs=[
                    whole(square),
                    whole((width, rows)),
                    whole(square),
                    whole((width, rows)),
                    whole((steps, 2 * lane)),
                    ANY,
                    ANY,
                ]
                + [whole(square)] * len(extra),
                out_specs=[
                    whole_out(square),
                    whole_out(square),
                    whole_out((steps, 2 * lane)),
                    ANY,
                    ANY,
                ],
                scratch_shapes=[
                    pltpu.VMEM((steps, width, 2 * lane), BF),
                    pltpu.VMEM((steps, width, 2 * lane), BF),
                    pltpu.VMEM((steps, width, 2 * lane), BF),
                    pltpu.VMEM((steps, width, 2 * lane), BF),
                    pltpu.SemaphoreType.DMA((PIECES,)),
                ],
            ),
            out_shape=[
                sds(square, F32),
                sds(square, F32),
                sds((steps, 2 * lane), F32),
                sds((HALF, 2 * depth, 2 * lane), BF),
                sds((HALF, 2 * depth, 2 * lane), BF),
            ],
            compiler_params=params(),
            cost_estimate=cost(12 * rows * width * part, 20 * rows * width),
            name="feed_forward",
        )(
            dest,
            second,
            second_t,
            dfeed,
            dfeed_t,
            up_rows[j],
            own_feed,
            other_feed,
            *extra,
        )
        up_sums.append(bias_sum.reshape(ROW_TILES, lane))
        feed_grads.append((keep, send))

    block_out, dresid, dattended, out_grad, middle_sums = pl.pallas_call(
        middle_kernel,
        grid_spec=pltpu.PrefetchScalarGridSpec(
            num_scalar_prefetch=1,
            grid=(images_here,),
            in_specs=[
                image_block,
                row_block,
                row_block,
                row_block,
                row_block,
                column_block,
                whole((width, width)),
                table_spec,
            ],
            out_specs=[
                image_block,
                row_block,
                column_block,
                whole_out((width, width)),
                whole_out((8, width)),
            ],
            scratch_shapes=[pltpu.VMEM((width, width), F32)],
        ),
        out_shape=[
            sds(images.shape, BF),
            sds((rows, width), F32),
            sds((width, rows), BF),
            sds((width, width), BF),
            sds((8, width), F32),
        ],
        compiler_params=params(),
        cost_estimate=cost(4 * rows * width * width, 30 * rows * width),
        name="middle",
    )(counts, cotangent, feed, dsecond, resid, branch, attended, out_full, table)

    dmixed, attention_sums = pl.pallas_call(
        attention_back_kernel,
        grid=(images_here,),
        in_specs=[mixed_block, probs_block, column_block, column_block],
        out_specs=[mixed_block, whole_out((8, width))],
        scratch_shapes=[pltpu.VMEM((width, 128), F32), pltpu.VMEM((width, 128), F32)],
        out_shape=[sds((3 * width, rows), BF), sds((8, width), F32)],
        compiler_params=params(),
        cost_estimate=cost(32 * rows * width * length, 18 * rows * width),
        name="attention_back",
    )(mixed, probs, attended, dattended)

    keep_first, send_first = pl.pallas_call(
        joint_grad_kernel,
        grid_spec=pltpu.PrefetchScalarGridSpec(
            num_scalar_prefetch=1,
            grid=(COL_TILES,),
            in_specs=[
                whole((width, rows)),
                pl.BlockSpec((span, rows), lambda s, *_: (s, 0)),
                whole((width, width)),
            ],
            out_specs=[ANY, ANY],
            scratch_shapes=[
                pltpu.VMEM((COL_TILES, width, width), BF),
                pltpu.SemaphoreType.DMA((PIECES,)),
            ],
        ),
        out_shape=[sds((HALF, depth, width), BF), sds((HALF, depth, width), BF)],
        compiler_params=params(),
        cost_estimate=cost(6 * rows * width * width, 10 * rows * width),
        name="joint_grad",
    )(dest, first_t, dmixed, out_grad)

    image_grad, input_sums = pl.pallas_call(
        input_grad_kernel,
        grid_spec=pltpu.PrefetchScalarGridSpec(
            num_scalar_prefetch=1,
            grid=(images_here,),
            in_specs=[image_block, row_block, mixed_block, table_spec, ANY, ANY],
            out_specs=[image_block, whole_out((8, width))],
            scratch_shapes=joint_scratch,
        ),
        out_shape=[sds(images.shape, F32), sds((8, width), F32)],
        compiler_params=params(),
        cost_estimate=cost(6 * rows * width * width, 20 * rows * width),
        name="input_grad",
    )(dest, images, dresid, dmixed, table, own_first, other_first)

    up_bias_grad = jnp.stack(up_sums, axis=1).reshape(-1)
    sums = jnp.concatenate(
        [
            input_sums[0:2],
            attention_sums[0:2],
            middle_sums[0:6],
            up_bias_grad.reshape(-1, width),
            jnp.zeros((2, width), F32),
        ]
    )
    short = first_gain.shape[0]
    if cube is not None:
        first_total = cube.reduce(keep_first, send_first)
        feed_total = cube.reduce(
            jnp.concatenate([k for k, _ in feed_grads], axis=1),
            jnp.concatenate([s for _, s in feed_grads], axis=1),
        )
        joint_grad, out_weight_grad = first_total[:, :span], first_total[:, span:]
        feed_total = feed_total.reshape(PARTS, 2, depth, 2, lane)
        up_grad = feed_total[:, 0].transpose(1, 2, 0, 3).reshape(up_weight.shape)
        down_grad = feed_total[:, 1].transpose(2, 1, 0, 3).reshape(down_weight.shape[::-1]).T
        sums = cube.total(sums)
        device = lax.axis_index("fsdp") * sub + lax.axis_index("sub")
        vectors = lax.dynamic_slice(sums[:10], (0, device * short), (10, short))
        up_bias_grad = lax.dynamic_slice(
            sums[10:14].reshape(-1), (device * up_bias.shape[0],), up_bias.shape
        )
    else:

        def hand_out(value):
            value = lax.psum_scatter(value.astype(BF), "fsdp", scatter_dimension=0, tiled=True)
            value = lax.psum_scatter(value, "sub", scatter_dimension=1, tiled=True)
            return value.astype(F32)

        def join(value, columns):
            value = value.reshape(ROW_TILES, COL_TILES, depth, columns)
            return value.transpose(0, 2, 1, 3).reshape(width, COL_TILES * columns)

        grads = jnp.concatenate([keep_first, send_first])
        joint_grad = hand_out(join(grads[:, :, :span], span))
        out_weight_grad = hand_out(join(grads[:, :, span:], piece))
        grads = jnp.stack([jnp.concatenate(pair) for pair in feed_grads], axis=1)
        grads = grads.reshape(ROW_TILES, COL_TILES, PARTS, 2, depth, 2, lane)
        up_grad = grads[:, :, :, 0].transpose(0, 3, 1, 4, 2, 5).reshape(width, hidden_units)
        down_grad = grads[:, :, :, 1].transpose(0, 2, 5, 1, 4, 3).reshape(hidden_units, width)
        up_grad, down_grad = hand_out(up_grad), hand_out(down_grad)

        def hand_vector(value):
            return lax.psum_scatter(value, BOTH, scatter_dimension=0, tiled=True)

        vectors = [hand_vector(sums[v]) for v in range(10)]
        up_bias_grad = hand_vector(up_bias_grad)
    return (
        block_out,
        image_grad,
        joint_grad,
        out_weight_grad,
        up_grad,
        down_grad,
        vectors[0],
        vectors[1],
        vectors[2],
        vectors[3],
        vectors[4],
        vectors[5],
        vectors[6],
        vectors[7],
        up_bias_grad,
        vectors[8],
        vectors[9],
    )


def solution(mesh):
    rows = P(BOTH, None, None)
    matrix = P("fsdp", "sub")
    vector = P(BOTH)
    sizes = (mesh.shape["fsdp"], mesh.shape["sub"])
    return jax.shard_map(
        functools.partial(shards, sizes=sizes),
        mesh=mesh,
        in_specs=(rows, vector) + (matrix,) * 4 + (vector,) * 11 + (rows,),
        out_specs=(rows, rows) + (matrix,) * 4 + (vector,) * 11,
        check_vma=False,
    )
```

time: 799 us -> 426 us (0.53)
  waiting for transfers between devices: 369 us -> 156 us
  Pallas kernels: 0 us -> 173 us
  matrix products: 151 us -> 0.21 us
  blocking collectives: 146 us -> 0 us
  starting transfers between devices: 0.75 us -> 46 us
  local copies, waits for them, and re-layouts: 62 us -> 24.4 us
  other arithmetic: 42.2 us -> 18.6 us
  between operations: 20.1 us -> 1.83 us
    reduce_scatter x5 -> x0, waiting for transfers between devices: 242 us -> none  [the longest x1 93.4 us: shards(): lax.psum_scatter(down_grad.astype(jnp.bfloat16), 'fsdp', scatter_dimensio...]
    pallas_call x0 -> x10, Pallas kernels: none -> 173 us  [the longest x3 77.7 us: shards(): pl.pallas_call(functools.partial(mlp_kernel, start, 1, j * 2 * depth), gr...]
    ppermute x0 -> x35, waiting for transfers between devices: none -> 156 us  [swap(): return lax.ppermute(value, BOTH, pairs)]
    dot_general x18 -> x1, matrix products: 151 us -> 0.21 us  [dot(): return jnp.dot(left, right, preferred_element_type=F32)]
    unnamed x4 -> x0, blocking collectives: 89.1 us -> none
    all_gather x4 -> x0, waiting for transfers between devices: 65.5 us -> none  [the longest x1 43.6 us: shards(): lax.all_gather(columns[3], 'fsdp', axis=0, tiled=True)]
    unnamed x15 -> x0, waiting for transfers between devices: 62.1 us -> none
    all_gather x5 -> x0, blocking collectives: 57 us -> none  [the longest x1 26.3 us: shards(): lax.all_gather(columns[12], 'fsdp', axis=0, tiled=True)]
  transfers between devices with their start and end apart: 12 -> 35, of which waited for: 10 -> 22; matrix products, arithmetic and copies ran while one was open for 24% -> 7% of each run, Pallas kernels for 0% -> 23%
where the time goes in v1:
time: 426 us; the launch traced here: 420 us
  Pallas kernels  173 us (41%)
  waiting for transfers between devices  156 us (37%)
  starting transfers between devices  46 us (11%)
  local copies, waits for them, and re-layouts  24.4 us (6%)
  other arithmetic  18.6 us (4%)
    ppermute x35, waiting for transfers between devices, swap(): return lax.ppermute(value, BOTH, pairs)  156 us
    pallas_call x3, Pallas kernels, shards(): pl.pallas_call(functools.partial(mlp_kernel, start, 1, j * 2 * depth), gr...  77.7 us
    ppermute x35, starting transfers between devices, swap(): return lax.ppermute(value, BOTH, pairs)  46 us
    pallas_call x1, Pallas kernels, shards(): pl.pallas_call(attention_kernel, grid_spec=pltpu.PrefetchScalarGridSpec(n...  18.8 us
    pallas_call x1, Pallas kernels, shards(): pl.pallas_call(attention_back_kernel, grid=(images_here,), in_specs=[mixe...  14.3 us
    pallas_call x1, Pallas kernels, shards(): pl.pallas_call(input_grad_kernel, grid_spec=pltpu.PrefetchScalarGridSpec(...  13.3 us
    pallas_call x1, Pallas kernels, shards(): pl.pallas_call(middle_kernel, grid_spec=pltpu.PrefetchScalarGridSpec(num_...  13.2 us
    pallas_call x1, Pallas kernels, shards(): pl.pallas_call(qkv_kernel, grid_spec=pltpu.PrefetchScalarGridSpec(num_sca...  12.5 us
  transfers between devices with their start and end apart: 35, of which 22 were waited for; matrix products, arithmetic and copies ran while one was open for 7% of the time, Pallas kernels for 23%

profile of v1, /device:TPU:0, one launch (start us, length us, event | category | flops | bytes accessed | tf_op | source)
XLA Modules:
  0.0 420.0 jit_solution(17925050057762497513)
XLA Ops:
  3.9 3.1 collective-permute-start.12
  7.0 2.6 collective-permute-start.13
  9.6 10.0 %collective-permute-done.12 = bf16[576,256]{1,0:T(8,128)(2,1)S(1)} collective-permute-done((bf16[576,256]{1,0:T(8,128)(2,1)S(1)}, bf16[576,256]{1,0:T(8,128)(2,1)S(1)}, u32[]{:S(2)}, u32[]{:S(2)}) %collective-permute-start.12) | collective-permute-done | bytes 294944 | tf_op jit(solution)/shard_map/ppermute | solution.py:461
  19.5 10.9 %collective-permute-done.13 = bf16[576,256]{1,0:T(8,128)(2,1)S(1)} collective-permute-done((bf16[576,256]{1,0:T(8,128)(2,1)S(1)}, bf16[576,256]{1,0:T(8,128)(2,1)S(1)}, u32[]{:S(2)}, u32[]{:S(2)}) %collective-permute-start.13) | collective-permute-done | bytes 294944 | tf_op jit(solution)/shard_map/ppermute | solution.py:461
  30.6 1.6 collective-permute-start.15
  35.2 11.7 %collective-permute-done.15 = bf16[4,576,256]{2,1,0:T(8,128)(2,1)S(1)} collective-permute-done((bf16[4,576,256]{2,1,0:T(8,128)(2,1)S(1)}, bf16[4,576,256]{2,1,0:T(8,128)(2,1)S(1)}, u32[]{:S(2)}, u32[]{:S(2)}) %collective-permute-start.15) | collective-permute-done | bytes 1179680 | tf_op jit(solution)/shard_map/ppermute | solution.py:461
  49.6 5.5 %collective-permute-start.6 = (bf16[96,768]{1,0:T(8,128)(2,1)S(1)}, bf16[96,768]{1,0:T(8,128)(2,1)S(1)}, u32[]{:S(2)}, u32[]{:S(2)}) collective-permute-start(bf16[96,768]{1,0:T(8,128)(2,1)S(1)} %get-tuple-element.98), channel_id=1, source_target_pairs={{0,8},{1,9},{2,10},{3,11},{4,12},{5,13},{6,14},{7,15},{8,0},{9,1},... | collective-permute-start | bytes 442376 | tf_op jit(solution)/shard_map/ppermute | solution.py:461
  57.6 1.6 collective-permute-done.6
  59.2 7.8 %collective-permute-done.7 = bf16[96,768]{1,0:T(8,128)(2,1)S(1)} collective-permute-done((bf16[96,768]{1,0:T(8,128)(2,1)S(1)}, bf16[96,768]{1,0:T(8,128)(2,1)S(1)}, u32[]{:S(2)}, u32[]{:S(2)}) %collective-permute-start.7) | collective-permute-done | bytes 147488 | tf_op jit(solution)/shard_map/ppermute | solution.py:461
  67.8 15.4 %collective-permute-done.16 = bf16[8,576,256]{2,1,0:T(8,128)(2,1)S(1)} collective-permute-done((bf16[8,576,256]{2,1,0:T(8,128)(2,1)S(1)}, bf16[8,576,256]{2,1,0:T(8,128)(2,1)S(1)}, u32[]{:S(2)}, u32[]{:S(2)}) %collective-permute-start.16) | collective-permute-done | bytes 2359328 | tf_op jit(solution)/shard_map/ppermute | solution.py:461
  83.2 1.6 constant_dynamic-update-slice_fusion.33.own
  85.1 1.6 collective-permute-start.10
  86.6 14.7 %collective-permute-done.10 = bf16[8,96,768]{2,1,0:T(8,128)(2,1)S(1)} collective-permute-done((bf16[8,96,768]{2,1,0:T(8,128)(2,1)S(1)}, bf16[8,96,768]{2,1,0:T(8,128)(2,1)S(1)}, u32[]{:S(2)}, u32[]{:S(2)}) %collective-permute-start.10) | collective-permute-done | bytes 1179680 | tf_op jit(solution)/shard_map/ppermute | solution.py:461
  101.8 5.5 %collective-permute-start = (bf16[8,128]{1,0:T(8,128)(2,1)S(1)}, bf16[8,128]{1,0:T(8,128)(2,1)S(1)}, u32[]{:S(2)}, u32[]{:S(2)}) collective-permute-start(bf16[8,128]{1,0:T(8,128)(2,1)S(1)} %get-tuple-element.167), channel_id=1, source_target_pairs={{0,8},{1,9},{2,10},{3,11},{4,12},{5,13},{6,14},{7,15},{8,0},{9,1},... | collective-permute-start | bytes 6152 | tf_op jit(solution)/shard_map/ppermute | solution.py:461
  109.8 2.0 collective-permute-done.1
  111.8 2.0 collective-permute-done.2
  113.8 1.6 collective-permute-start.3
  115.4 2.1 collective-permute-done.3
  119.0 2.2 collective-permute-done.4
  127.9 12.5 %qkv.1 = (bf16[2304,1024]{1,0:T(8,128)(2,1)}, bf16[768,1024]{1,0:T(8,128)(2,1)}) custom-call(s32[32]{0:T(128)} %add_add_fusion.dest, bf16[4,256,768]{2,1,0:T(8,128)(2,1)} %images.5, f32[10,768]{1,0:T(8,128)} %stack.52.table, f32[4,768]{1,0:T(4,128)} %pad.9.bias, bf16[16,96,768]{2,1,0:T(8,128)(2,1)} %copy-done, bf16[16,96,768]{2,1,0:T(8,128)(2,1)} %collective-permute-done.11.other), custom_call_target="tpu_custom_call" | custom-call | flops 3623878656 | bytes 11010048 | tf_op jit(solution)/shard_map/qkv/pallas_call | solution.py:673
  140.4 18.8 %attention.1 = (bf16[768,1024]{1,0:T(8,128)(2,1)}, bf16[4,12,256,256]{3,2,1,0:T(8,128)(2,1)}) custom-call(s32[4]{0:T(128)} %counts.5, bf16[2304,1024]{1,0:T(8,128)(2,1)} %get-tuple-element.54.mixed), custom_call_target="tpu_custom_call" | custom-call | flops 3221225472 | bytes 6291456 | tf_op jit(solution)/shard_map/attention/pallas_call | solution.py:688
  159.2 11.5 %second_norm.1 = (f32[1024,768]{1,0:T(8,128)}, bf16[1024,768]{1,0:T(8,128)(2,1)}, bf16[1024,768]{1,0:T(8,128)(2,1)}, bf16[768,1024]{1,0:T(8,128)(2,1)}, bf16[102...) custom-call(s32[32]{0:T(128)} %add_add_fusion.dest, s32[4]{0:T(128)} %counts.5, ...), custom_call_target="tpu_custom_call" | custom-call | flops 1207959552 | bytes 15728640 | tf_op jit(solution)/shard_map/second_norm/pallas_call | solution.py:705
  170.7 24.6 %feed_forward.3 = (f32[1024,768]{1,0:T(8,128)}, f32[1024,768]{1,0:T(8,128)}, f32[4,256]{1,0:T(4,128)}, bf16[16,192,256]{2,1,0:T(8,128)(2,1)}, bf16[16,192,256]{2,1,0:T(8,128)(2,1)}) custom-call(s32[32]{0:T(128)} %add_add_fusion.dest, bf16[1024,768]{1,0:T(8,128)(2,1)} %get-tuple-element.56.second, bf16[768,1024]{1,0:T(8,128)(2,1)} %get-tuple-element.57.second_t, ...), custom_call_target="tpu_custom_call" | custom-call | flops 9663676416 | bytes 15728640 | tf_op jit(solution)/shard_map/feed_forward/pallas_call | solution.py:743
  195.3 26.5 %feed_forward.4 = (f32[1024,768]{1,0:T(8,128)}, f32[1024,768]{1,0:T(8,128)}, f32[4,256]{1,0:T(4,128)}, bf16[16,192,256]{2,1,0:T(8,128)(2,1)}, bf16[16,192,256]{2,1,0:T(8,128)(2,1)}) custom-call(s32[32]{0:T(128)} %add_add_fusion.dest, bf16[1024,768]{1,0:T(8,128)(2,1)} %get-tuple-element.56.second, bf16[768,1024]{1,0:T(8,128)(2,1)} %get-tuple-element.57.second_t, ...), custom_call_target="tpu_custom_call" | custom-call | flops 9663676416 | bytes 15728640 | tf_op jit(solution)/shard_map/feed_forward/pallas_call | solution.py:743
  221.8 26.6 %feed_forward.5 = (f32[1024,768]{1,0:T(8,128)}, f32[1024,768]{1,0:T(8,128)}, f32[4,256]{1,0:T(4,128)}, bf16[16,192,256]{2,1,0:T(8,128)(2,1)}, bf16[16,192,256]{2,1,0:T(8,128)(2,1)}) custom-call(s32[32]{0:T(128)} %add_add_fusion.dest, bf16[1024,768]{1,0:T(8,128)(2,1)} %get-tuple-element.56.second, bf16[768,1024]{1,0:T(8,128)(2,1)} %get-tuple-element.57.second_t, ...), custom_call_target="tpu_custom_call" | custom-call | flops 9663676416 | bytes 15728640 | tf_op jit(solution)/shard_map/feed_forward/pallas_call | solution.py:743
  248.4 3.4 pad_maximum_fusion
  252.0 13.2 %middle.1 = (bf16[4,256,768]{2,1,0:T(8,128)(2,1)}, f32[1024,768]{1,0:T(8,128)}, bf16[768,1024]{1,0:T(8,128)(2,1)}, bf16[768,768]{1,0:T(8,128)(2,1)}, f32[8,768]{1,0:T(8,128)}) custom-call(s32[4]{0:T(128)} %counts.5, bf16[4,256,768]{2,1,0:T(8,128)(2,1)} %cotangent.3, f32[1024,768]{1,0:T(8,128)} %get-tuple-element.64.feed, ...), custom_call_target="tpu_custom_call" | custom-call | flops 2415919104 | bytes 23592960 | tf_op jit(solution)/shard_map/middle/pallas_call | solution.py:797
  265.3 14.3 %attention_back.1 = (bf16[2304,1024]{1,0:T(8,128)(2,1)}, f32[8,768]{1,0:T(8,128)}) custom-call(bf16[2304,1024]{1,0:T(8,128)(2,1)} %get-tuple-element.54.mixed, bf16[4,12,256,256]{3,2,1,0:T(8,128)(2,1)} %get-tuple-element.71.probs, bf16[768,1024]{1,0:T(8,128)(2,1)} %get-tuple-element.55.attended, bf16[768,1024]{1,0:T(8,128)(2,1)} %get-tuple-element.72.dattended), custom_call_target="tpu_custom_call" | custom-call | flops 6442450944 | bytes 14155776 | tf_op jit(solution)/shard_map/attention_back/pallas_call | solution.py:833
  279.5 11.4 %joint_grad.1 = (bf16[16,96,768]{2,1,0:T(8,128)(2,1)}, bf16[16,96,768]{2,1,0:T(8,128)(2,1)}) custom-call(s32[32]{0:T(128)} %add_add_fusion.dest, bf16[768,1024]{1,0:T(8,128)(2,1)} %get-tuple-element.75.first_t, bf16[2304,1024]{1,0:T(8,128)(2,1)} %get-tuple-element.73.dmixed, bf16[768,768]{1,0:T(8,128)(2,1)} %get-tuple-element.76.out_grad), custom_call_target="tpu_custom_call" | custom-call | flops 3623878656 | bytes 7864320 | tf_op jit(solution)/shard_map/joint_grad/pallas_call | solution.py:845
  293.1 2.2 add_convert_fusion.1
  296.8 1.7 add_convert_fusion.5
  299.1 25.4 %collective-permute-done.25 = bf16[8,576,256]{2,1,0:T(8,128)(2,1)} collective-permute-done((bf16[8,576,256]{2,1,0:T(8,128)(2,1)}, bf16[8,576,256]{2,1,0:T(8,128)(2,1)}, u32[]{:S(2)}, u32[]{:S(2)}) %collective-permute-start.25) | collective-permute-done | bytes 2359328 | tf_op jit(solution)/shard_map/ppermute | solution.py:461
  324.5 3.6 add_convert_fusion.3
  329.6 14.2 %collective-permute-done.19 = bf16[8,96,768]{2,1,0:T(8,128)(2,1)} collective-permute-done((bf16[8,96,768]{2,1,0:T(8,128)(2,1)}, bf16[8,96,768]{2,1,0:T(8,128)(2,1)}, u32[]{:S(2)}, u32[]{:S(2)}) %collective-permute-start.19) | collective-permute-done | bytes 1179680 | tf_op jit(solution)/shard_map/ppermute | solution.py:461
  343.8 1.5 add_convert_fusion.7
  345.3 1.6 collective-permute-start.20
  346.9 13.3 %input_grad.1 = (f32[4,256,768]{2,1,0:T(8,128)}, f32[8,768]{1,0:T(8,128)}) custom-call(s32[32]{0:T(128)} %add_add_fusion.dest, bf16[4,256,768]{2,1,0:T(8,128)(2,1)} %images.5, f32[1024,768]{1,0:T(8,128)} %get-tuple-element.70.dresid, bf16[2304,1024]{1,0:T(8,128)(2,1)} %get-tuple-element.73.dmixed, f32[10,768]{1,0:T(8,128)} %stack.52.table, ...), custom_call_target="tpu_custom_call" | custom-call | flops 3623878656 | bytes 15728640 | tf_op jit(solution)/shard_map/input_grad/pallas_call | solution.py:867
  363.3 1.5 collective-permute-start.31
  364.8 2.6 collective-permute-done.31
  368.0 3.6 collective-permute-done.32
  371.8 3.9 collective-permute-done.33
  375.8 5.6 %collective-permute-done.34 = f32[16,768]{1,0:T(8,128)S(1)} collective-permute-done((f32[16,768]{1,0:T(8,128)S(1)}, f32[16,768]{1,0:T(8,128)S(1)}, u32[]{:S(2)}, u32[]{:S(2)}) %collective-permute-start.34) | collective-permute-done | bytes 49184 | tf_op jit(solution)/shard_map/ppermute | solution.py:461
  383.7 2.9 collective-permute-start.23
  386.7 2.1 fusion.3
  390.2 1.6 collective-permute-done.21
  391.8 1.9 collective-permute-start.29
  398.7 2.8 collective-permute-done.27
  401.5 14.3 %collective-permute-done.28 = bf16[576,256]{1,0:T(8,128)(2,1)S(1)} collective-permute-done((bf16[576,256]{1,0:T(8,128)(2,1)S(1)}, bf16[576,256]{1,0:T(8,128)(2,1)S(1)}, u32[]{:S(2)}, u32[]{:S(2)}) %collective-permute-start.28) | collective-permute-done | bytes 294944 | tf_op jit(solution)/shard_map/ppermute | solution.py:461
  (190 shorter events, 45.7 us)
Async XLA Ops:
  3.9 15.6 %collective-permute-start.12 = (bf16[576,256]{1,0:T(8,128)(2,1)S(1)}, bf16[576,256]{1,0:T(8,128)(2,1)S(1)}, u32[]{:S(2)}, u32[]{:S(2)}) collective-permute-start(bf16[576,256]{1,0:T(8,128)(2,1)S(1)} %constant_dynamic-update-slice_fusion.22), channel_id=1, source_target_pairs={{0,8},{1,9},{2,10},{3,11},{4,12},{5,13},{6,14},{7,15},{8,0},{9,1},... | collective-permute-start | bytes 884744 | tf_op jit(solution)/shard_map/ppermute | solution.py:461
  7.0 23.5 %collective-permute-start.13 = (bf16[576,256]{1,0:T(8,128)(2,1)S(1)}, bf16[576,256]{1,0:T(8,128)(2,1)S(1)}, u32[]{:S(2)}, u32[]{:S(2)}) collective-permute-start(bf16[576,256]{1,0:T(8,128)(2,1)S(1)} %constant_dynamic-update-slice_fusion.22), channel_id=1, source_target_pairs={{0,16},{1,17},{2,18},{3,19},{4,20},{5,21},{6,22},{7,23},{8,24},{9,... | collective-permute-start | bytes 884744 | tf_op jit(solution)/shard_map/ppermute | solution.py:461
  9.6 20.9 %collective-permute-start.14 = (bf16[576,256]{1,0:T(8,128)(2,1)S(1)}, bf16[576,256]{1,0:T(8,128)(2,1)S(1)}, u32[]{:S(2)}, u32[]{:S(2)}) collective-permute-start(bf16[576,256]{1,0:T(8,128)(2,1)S(1)} %constant_dynamic-update-slice_fusion.22), channel_id=1, source_target_pairs={{0,24},{1,25},{2,26},{3,27},{4,28},{5,29},{6,30},{7,31},{8,16},{9,... | collective-permute-start | bytes 884744 | tf_op jit(solution)/shard_map/ppermute | solution.py:461
  30.6 16.3 %collective-permute-start.15 = (bf16[4,576,256]{2,1,0:T(8,128)(2,1)S(1)}, bf16[4,576,256]{2,1,0:T(8,128)(2,1)S(1)}, u32[]{:S(2)}, u32[]{:S(2)}) collective-permute-start(bf16[4,576,256]{2,1,0:T(8,128)(2,1)S(1)} %pad_maximum_fusion.1), channel_id=1, source_target_pairs={{0,4},{1,3},{2,6},{3,1},{4,0},{5,7},{6,2},{7,5},{8,12},{9,11},{10,... | collective-permute-start | bytes 3538952 | tf_op jit(solution)/shard_map/ppermute | solution.py:461
  48.0 35.2 %collective-permute-start.16 = (bf16[8,576,256]{2,1,0:T(8,128)(2,1)S(1)}, bf16[8,576,256]{2,1,0:T(8,128)(2,1)S(1)}, u32[]{:S(2)}, u32[]{:S(2)}) collective-permute-start(bf16[8,576,256]{2,1,0:T(8,128)(2,1)S(1)} %get-tuple-element.113), channel_id=1, source_target_pairs={{0,2},{1,5},{2,0},{3,7},{4,6},{5,1},{6,4},{7,3},{8,10},{9,13},{10,... | collective-permute-start | bytes 7077896 | tf_op jit(solution)/shard_map/ppermute | solution.py:461
  49.6 9.6 %collective-permute-start.6 = (bf16[96,768]{1,0:T(8,128)(2,1)S(1)}, bf16[96,768]{1,0:T(8,128)(2,1)S(1)}, u32[]{:S(2)}, u32[]{:S(2)}) collective-permute-start(bf16[96,768]{1,0:T(8,128)(2,1)S(1)} %get-tuple-element.98), channel_id=1, source_target_pairs={{0,8},{1,9},{2,10},{3,11},{4,12},{5,13},{6,14},{7,15},{8,0},{9,1},... | collective-permute-start | bytes 442376 | tf_op jit(solution)/shard_map/ppermute | solution.py:461
  55.2 11.9 %collective-permute-start.7 = (bf16[96,768]{1,0:T(8,128)(2,1)S(1)}, bf16[96,768]{1,0:T(8,128)(2,1)S(1)}, u32[]{:S(2)}, u32[]{:S(2)}) collective-permute-start(bf16[96,768]{1,0:T(8,128)(2,1)S(1)} %get-tuple-element.98), channel_id=1, source_target_pairs={{0,16},{1,17},{2,18},{3,19},{4,20},{5,21},{6,22},{7,23},{8,24},{9,... | collective-permute-start | bytes 442376 | tf_op jit(solution)/shard_map/ppermute | solution.py:461
  56.2 10.8 %collective-permute-start.8 = (bf16[96,768]{1,0:T(8,128)(2,1)S(1)}, bf16[96,768]{1,0:T(8,128)(2,1)S(1)}, u32[]{:S(2)}, u32[]{:S(2)}) collective-permute-start(bf16[96,768]{1,0:T(8,128)(2,1)S(1)} %get-tuple-element.98), channel_id=1, source_target_pairs={{0,24},{1,25},{2,26},{3,27},{4,28},{5,29},{6,30},{7,31},{8,16},{9,... | collective-permute-start | bytes 442376 | tf_op jit(solution)/shard_map/ppermute | solution.py:461
  67.1 17.9 %collective-permute-start.9 = (bf16[4,96,768]{2,1,0:T(8,128)(2,1)S(1)}, bf16[4,96,768]{2,1,0:T(8,128)(2,1)S(1)}, u32[]{:S(2)}, u32[]{:S(2)}) collective-permute-start(bf16[4,96,768]{2,1,0:T(8,128)(2,1)S(1)} %pad_maximum_fusion.2), channel_id=1, source_target_pairs={{0,4},{1,3},{2,6},{3,1},{4,0},{5,7},{6,2},{7,5},{8,12},{9,11},{10,... | collective-permute-start | bytes 1769480 | tf_op jit(solution)/shard_map/ppermute | solution.py:461
  84.8 16.8 %copy-start.16 = (bf16[24]{0:T(256)(128)(2,1)S(1)}, bf16[24]{0:T(256)(128)(2,1)}, u32[]{:S(2)}) copy-start(bf16[24]{0:T(256)(128)(2,1)} %param.26) | copy-start | bytes 148
  84.8 16.8 %copy-start.17 = (bf16[24]{0:T(256)(128)(2,1)S(1)}, bf16[24]{0:T(256)(128)(2,1)}, u32[]{:S(2)}) copy-start(bf16[24]{0:T(256)(128)(2,1)} %param.27) | copy-start | bytes 148
  84.8 16.8 %copy-start.18 = (bf16[24]{0:T(256)(128)(2,1)S(1)}, bf16[24]{0:T(256)(128)(2,1)}, u32[]{:S(2)}) copy-start(bf16[24]{0:T(256)(128)(2,1)} %param.28) | copy-start | bytes 148
  84.8 16.8 %copy-start.19 = (bf16[24]{0:T(256)(128)(2,1)S(1)}, bf16[24]{0:T(256)(128)(2,1)}, u32[]{:S(2)}) copy-start(bf16[24]{0:T(256)(128)(2,1)} %param.29) | copy-start | bytes 148
  84.8 16.8 %copy-start.20 = (bf16[24]{0:T(256)(128)(2,1)S(1)}, bf16[24]{0:T(256)(128)(2,1)}, u32[]{:S(2)}) copy-start(bf16[24]{0:T(256)(128)(2,1)} %param.30) | copy-start | bytes 148
  84.8 16.8 %copy-start.21 = (bf16[24]{0:T(256)(128)(2,1)S(1)}, bf16[24]{0:T(256)(128)(2,1)}, u32[]{:S(2)}) copy-start(bf16[24]{0:T(256)(128)(2,1)} %param.31) | copy-start | bytes 148
  84.8 16.8 %copy-start.22 = (bf16[96]{0:T(256)(128)(2,1)S(1)}, bf16[96]{0:T(256)(128)(2,1)}, u32[]{:S(2)}) copy-start(bf16[96]{0:T(256)(128)(2,1)} %param.32) | copy-start | bytes 580
  84.9 16.8 %copy-start.23 = (bf16[24]{0:T(256)(128)(2,1)S(1)}, bf16[24]{0:T(256)(128)(2,1)}, u32[]{:S(2)}) copy-start(bf16[24]{0:T(256)(128)(2,1)} %param.33) | copy-start | bytes 148
  84.9 16.8 %copy-start.24 = (bf16[24]{0:T(256)(128)(2,1)S(1)}, bf16[24]{0:T(256)(128)(2,1)}, u32[]{:S(2)}) copy-start(bf16[24]{0:T(256)(128)(2,1)} %param.34) | copy-start | bytes 148
  84.9 85.8 %collective-permute-start.17 = (bf16[16,576,256]{2,1,0:T(8,128)(2,1)}, bf16[16,576,256]{2,1,0:T(8,128)(2,1)}, u32[]{:S(2)}, u32[]{:S(2)}) collective-permute-start(bf16[16,576,256]{2,1,0:T(8,128)(2,1)} %constant_dynamic-update-slice_fusion.33.own), channel_id=1, source_target_pairs={{0,1},{1,0},{2,3},{3,2},{4,5},{5,4},{6,7},{7,6},{8,9},{9,8},{10,11... | collective-permute-start | bytes 14155784 | tf_op jit(solution)/shard_map/ppermute | solution.py:461
  85.1 16.3 %collective-permute-start.10 = (bf16[8,96,768]{2,1,0:T(8,128)(2,1)S(1)}, bf16[8,96,768]{2,1,0:T(8,128)(2,1)S(1)}, u32[]{:S(2)}, u32[]{:S(2)}) collective-permute-start(bf16[8,96,768]{2,1,0:T(8,128)(2,1)S(1)} %get-tuple-element.117), channel_id=1, source_target_pairs={{0,2},{1,5},{2,0},{3,7},{4,6},{5,1},{6,4},{7,3},{8,10},{9,13},{10,... | collective-permute-start | bytes 3538952 | tf_op jit(solution)/shard_map/ppermute | solution.py:461
  101.4 26.4 %copy-start = (bf16[16,96,768]{2,1,0:T(8,128)(2,1)}, bf16[16,96,768]{2,1,0:T(8,128)(2,1)S(1)}, u32[]{:S(2)}) copy-start(bf16[16,96,768]{2,1,0:T(8,128)(2,1)S(1)} %constant_dynamic-update-slice_fusion.16.own) | copy-start | bytes 7077892
  101.4 26.4 %collective-permute-start.11 = (bf16[16,96,768]{2,1,0:T(8,128)(2,1)S(1)}, bf16[16,96,768]{2,1,0:T(8,128)(2,1)}, u32[]{:S(2)}, u32[]{:S(2)}) collective-permute-start(bf16[16,96,768]{2,1,0:T(8,128)(2,1)S(1)} %constant_dynamic-update-slice_fusion.16.own), channel_id=1, source_target_pairs={{0,1},{1,0},{2,3},{3,2},{4,5},{5,4},{6,7},{7,6},{8,9},{9,8},{10,11... | collective-permute-start | bytes 7077896 | tf_op jit(solution)/shard_map/ppermute | solution.py:461
  101.8 8.0 %collective-permute-start = (bf16[8,128]{1,0:T(8,128)(2,1)S(1)}, bf16[8,128]{1,0:T(8,128)(2,1)S(1)}, u32[]{:S(2)}, u32[]{:S(2)}) collective-permute-start(bf16[8,128]{1,0:T(8,128)(2,1)S(1)} %get-tuple-element.167), channel_id=1, source_target_pairs={{0,8},{1,9},{2,10},{3,11},{4,12},{5,13},{6,14},{7,15},{8,0},{9,1},... | collective-permute-start | bytes 6152 | tf_op jit(solution)/shard_map/ppermute | solution.py:461
  107.3 4.5 %collective-permute-start.1 = (bf16[8,128]{1,0:T(8,128)(2,1)S(1)}, bf16[8,128]{1,0:T(8,128)(2,1)S(1)}, u32[]{:S(2)}, u32[]{:S(2)}) collective-permute-start(bf16[8,128]{1,0:T(8,128)(2,1)S(1)} %get-tuple-element.167), channel_id=1, source_target_pairs={{0,16},{1,17},{2,18},{3,19},{4,20},{5,21},{6,22},{7,23},{8,24},{9,... | collective-permute-start | bytes 6152 | tf_op jit(solution)/shard_map/ppermute | solution.py:461
  108.4 5.4 %collective-permute-start.2 = (bf16[8,128]{1,0:T(8,128)(2,1)S(1)}, bf16[8,128]{1,0:T(8,128)(2,1)S(1)}, u32[]{:S(2)}, u32[]{:S(2)}) collective-permute-start(bf16[8,128]{1,0:T(8,128)(2,1)S(1)} %get-tuple-element.167), channel_id=1, source_target_pairs={{0,24},{1,25},{2,26},{3,27},{4,28},{5,29},{6,30},{7,31},{8,16},{9,... | collective-permute-start | bytes 6152 | tf_op jit(solution)/shard_map/ppermute | solution.py:461
  113.8 3.7 collective-permute-start.3
  117.5 3.7 collective-permute-start.4
  121.2 1.2 collective-permute-start.5
  221.8 26.7 %copy-start.3 = (bf16[16,192,256]{2,1,0:T(8,128)(2,1)S(1)}, bf16[16,192,256]{2,1,0:T(8,128)(2,1)}, u32[]{:S(2)}) copy-start(bf16[16,192,256]{2,1,0:T(8,128)(2,1)} %get-tuple-element.82) | copy-start | bytes 4718596
  221.8 26.7 %copy-start.4 = (bf16[16,192,256]{2,1,0:T(8,128)(2,1)S(1)}, bf16[16,192,256]{2,1,0:T(8,128)(2,1)}, u32[]{:S(2)}) copy-start(bf16[16,192,256]{2,1,0:T(8,128)(2,1)} %get-tuple-element.83) | copy-start | bytes 4718596
  251.9 41.3 %collective-permute-start.24 = (bf16[16,576,256]{2,1,0:T(8,128)(2,1)}, bf16[16,576,256]{2,1,0:T(8,128)(2,1)S(1)}, u32[]{:S(2)}, u32[]{:S(2)}) collective-permute-start(bf16[16,576,256]{2,1,0:T(8,128)(2,1)} %pad_maximum_fusion), channel_id=1, source_target_pairs={{0,1},{1,0},{2,3},{3,2},{4,5},{5,4},{6,7},{7,6},{8,9},{9,8},{10,11... | collective-permute-start | bytes 14155784 | tf_op jit(solution)/shard_map/ppermute | solution.py:461
  290.9 5.9 %collective-permute-start.18 = (bf16[16,96,768]{2,1,0:T(8,128)(2,1)}, bf16[16,96,768]{2,1,0:T(8,128)(2,1)S(1)}, u32[]{:S(2)}, u32[]{:S(2)}) collective-permute-start(bf16[16,96,768]{2,1,0:T(8,128)(2,1)} %get-tuple-element.78), channel_id=1, source_target_pairs={{0,1},{1,0},{2,3},{3,2},{4,5},{5,4},{6,7},{7,6},{8,9},{9,8},{10,11... | collective-permute-start | bytes 7077896 | tf_op jit(solution)/shard_map/ppermute | solution.py:461
  295.3 29.2 %collective-permute-start.25 = (bf16[8,576,256]{2,1,0:T(8,128)(2,1)}, bf16[8,576,256]{2,1,0:T(8,128)(2,1)}, u32[]{:S(2)}, u32[]{:S(2)}) collective-permute-start(bf16[8,576,256]{2,1,0:T(8,128)(2,1)} %get-tuple-element.100), channel_id=1, source_target_pairs={{0,2},{1,5},{2,0},{3,7},{4,6},{5,1},{6,4},{7,3},{8,10},{9,13},{10,... | collective-permute-start | bytes 7077896 | tf_op jit(solution)/shard_map/ppermute | solution.py:461
  298.5 45.2 %collective-permute-start.19 = (bf16[8,96,768]{2,1,0:T(8,128)(2,1)}, bf16[8,96,768]{2,1,0:T(8,128)(2,1)}, u32[]{:S(2)}, u32[]{:S(2)}) collective-permute-start(bf16[8,96,768]{2,1,0:T(8,128)(2,1)} %get-tuple-element.104), channel_id=1, source_target_pairs={{0,2},{1,5},{2,0},{3,7},{4,6},{5,1},{6,4},{7,3},{8,10},{9,13},{10,... | collective-permute-start | bytes 3538952 | tf_op jit(solution)/shard_map/ppermute | solution.py:461
  328.1 58.6 %collective-permute-start.26 = (bf16[4,576,256]{2,1,0:T(8,128)(2,1)}, bf16[4,576,256]{2,1,0:T(8,128)(2,1)}, u32[]{:S(2)}, u32[]{:S(2)}) collective-permute-start(bf16[4,576,256]{2,1,0:T(8,128)(2,1)} %get-tuple-element.102), channel_id=1, source_target_pairs={{0,4},{1,3},{2,6},{3,1},{4,0},{5,7},{6,2},{7,5},{8,12},{9,11},{10,... | collective-permute-start | bytes 3538952 | tf_op jit(solution)/shard_map/ppermute | solution.py:461
  345.3 36.2 %collective-permute-start.20 = (bf16[4,96,768]{2,1,0:T(8,128)(2,1)S(1)}, bf16[4,96,768]{2,1,0:T(8,128)(2,1)S(1)}, u32[]{:S(2)}, u32[]{:S(2)}) collective-permute-start(bf16[4,96,768]{2,1,0:T(8,128)(2,1)S(1)} %get-tuple-element.109), channel_id=1, source_target_pairs={{0,4},{1,3},{2,6},{3,1},{4,0},{5,7},{6,2},{7,5},{8,12},{9,11},{10,... | collective-permute-start | bytes 1769480 | tf_op jit(solution)/shard_map/ppermute | solution.py:461
  360.2 26.5 %copy-start.1 = (bf16[4,576,256]{2,1,0:T(8,128)(2,1)S(1)}, bf16[4,576,256]{2,1,0:T(8,128)(2,1)}, u32[]{:S(2)}) copy-start(bf16[4,576,256]{2,1,0:T(8,128)(2,1)} %get-tuple-element.101) | copy-start | bytes 3538948
  362.0 1.3 collective-permute-start.30
  363.3 4.1 collective-permute-start.31
  367.4 4.2 collective-permute-start.32
  371.6 4.2 collective-permute-start.33
  375.7 5.7 %collective-permute-start.34 = (f32[16,768]{1,0:T(8,128)S(1)}, f32[16,768]{1,0:T(8,128)S(1)}, u32[]{:S(2)}, u32[]{:S(2)}) collective-permute-start(f32[16,768]{1,0:T(8,128)S(1)} %add.247), channel_id=1, source_target_pairs={{0,16},{1,17},{2,18},{3,19},{4,20},{5,21},{6,22},{7,23},{8,24},{9,... | collective-permute-start | bytes 147464 | tf_op jit(solution)/shard_map/ppermute | solution.py:461
  382.3 9.5 %collective-permute-start.21 = (bf16[96,768]{1,0:T(8,128)(2,1)S(1)}, bf16[96,768]{1,0:T(8,128)(2,1)}, u32[]{:S(2)}, u32[]{:S(2)}) collective-permute-start(bf16[96,768]{1,0:T(8,128)(2,1)S(1)} %get-tuple-element.110), channel_id=1, source_target_pairs={{0,8},{1,9},{2,10},{3,11},{4,12},{5,13},{6,14},{7,15},{8,0},{9,1},... | collective-permute-start | bytes 442376 | tf_op jit(solution)/shard_map/ppermute | solution.py:461
  382.7 13.4 %collective-permute-start.22 = (bf16[96,768]{1,0:T(8,128)(2,1)}, bf16[96,768]{1,0:T(8,128)(2,1)}, u32[]{:S(2)}, u32[]{:S(2)}) collective-permute-start(bf16[96,768]{1,0:T(8,128)(2,1)} %get-tuple-element.112), channel_id=1, source_target_pairs={{0,16},{1,17},{2,18},{3,19},{4,20},{5,21},{6,22},{7,23},{8,24},{9,... | collective-permute-start | bytes 442376 | tf_op jit(solution)/shard_map/ppermute | solution.py:461
  383.7 12.4 %collective-permute-start.23 = (bf16[96,768]{1,0:T(8,128)(2,1)}, bf16[96,768]{1,0:T(8,128)(2,1)}, u32[]{:S(2)}, u32[]{:S(2)}) collective-permute-start(bf16[96,768]{1,0:T(8,128)(2,1)} %get-tuple-element.111), channel_id=1, source_target_pairs={{0,24},{1,25},{2,26},{3,27},{4,28},{5,29},{6,30},{7,31},{8,16},{9,... | collective-permute-start | bytes 442376 | tf_op jit(solution)/shard_map/ppermute | solution.py:461
  388.7 12.8 %collective-permute-start.27 = (bf16[576,256]{1,0:T(8,128)(2,1)}, bf16[576,256]{1,0:T(8,128)(2,1)S(1)}, u32[]{:S(2)}, u32[]{:S(2)}) collective-permute-start(bf16[576,256]{1,0:T(8,128)(2,1)} %get-tuple-element.105), channel_id=1, source_target_pairs={{0,8},{1,9},{2,10},{3,11},{4,12},{5,13},{6,14},{7,15},{8,0},{9,1},... | collective-permute-start | bytes 884744 | tf_op jit(solution)/shard_map/ppermute | solution.py:461
  388.7 27.1 %collective-permute-start.28 = (bf16[576,256]{1,0:T(8,128)(2,1)S(1)}, bf16[576,256]{1,0:T(8,128)(2,1)S(1)}, u32[]{:S(2)}, u32[]{:S(2)}) collective-permute-start(bf16[576,256]{1,0:T(8,128)(2,1)S(1)} %get-tuple-element.107), channel_id=1, source_target_pairs={{0,16},{1,17},{2,18},{3,19},{4,20},{5,21},{6,22},{7,23},{8,24},{9,... | collective-permute-start | bytes 884744 | tf_op jit(solution)/shard_map/ppermute | solution.py:461
  391.8 24.1 %collective-permute-start.29 = (bf16[576,256]{1,0:T(8,128)(2,1)S(1)}, bf16[576,256]{1,0:T(8,128)(2,1)}, u32[]{:S(2)}, u32[]{:S(2)}) collective-permute-start(bf16[576,256]{1,0:T(8,128)(2,1)S(1)} %get-tuple-element.106), channel_id=1, source_target_pairs={{0,24},{1,25},{2,26},{3,27},{4,28},{5,29},{6,30},{7,31},{8,16},{9,... | collective-permute-start | bytes 884744 | tf_op jit(solution)/shard_map/ppermute | solution.py:461
  (12 other events, 103.9 us)
